TPU v7x, 32 devices: a whole 2x2x4 slice. The times are simulated.
32 devices in a mesh: aux: 32 (over z, y, x, core), occ: 1.
Axes of the slice: x: 2, y: 2, z: 4, core: 2. Of those that a mesh axis runs over, the one named last changes fastest.
Arguments:
- ints: bfloat16 [32, 16, 16, 16384], P(None, None, None, 'aux'), may hold values from -0.125 to 0.125
- blk_atoms: int32 [1024, 2], P('aux'), may hold values from 0 to 255
- blk_count: int32 [32], P('aux'), may hold values from 1 to 32, as said below
- occ_coeff: bfloat16 [1280, 4096], P(None, 'occ'), may hold values from -1.5 to 1.5
- vir_coeff: bfloat16 [4096, 384], P(None, 'occ'), may hold values from -1.5 to 1.5
- batch_ids: int32 [8], replicated, may hold values from 0 to 1279, as said below
Outputs:
- pair_ints: float32 [8, 32, 12, 8, 12], P(None, 'aux', 'occ')
Inputs may be any that keep to these rules, and one draw needn't show every extreme that they name: `batch_ids`: the batch's orbitals are distinct, and the batch holds the last occupied orbital. `blk_count`: every owner has at least one live slot, and some owner has all 32 live. Slots of owner g name atoms within 2 * 256 // 32 (at least 2) atoms after atom g * 8, cyclically.
All inputs are finite; a program needn't handle non-finite values.
Results may differ from a plain program's by a relative error of at most 0.0017.
Values may be sent and summed in bfloat16 or wider, within the bound.
No kernel may reach another device: no remote copies, remote signals or barrier semaphores. Data moves between devices by JAX's collectives and lax.ppermute only.
A program may use at most 128 MiB of HBM per device.

v0:
```python
import jax
import jax.numpy as jnp
from jax import lax
from jax.sharding import PartitionSpec as P


def half_transform(left_rows, right_rows, block_ints, live_count):
    half_ints = jnp.einsum(
        "ikm,kmnq->kinq", left_rows, block_ints, preferred_element_type=jnp.float32
    )
    slot_ids = jnp.arange(block_ints.shape[0], dtype=jnp.int32)
    half_ints = jnp.where((slot_ids < live_count)[:, None, None, None], half_ints, 0.0).astype(
        jnp.bfloat16
    )
    return jnp.einsum("knv,kinq->ivq", right_rows, half_ints, preferred_element_type=jnp.float32)


def on_device(ints, blk_atoms, blk_count, occ_coeff, vir_coeff, batch_ids):
    batch_size = batch_ids.shape[0]
    block_size = ints.shape[1]
    aux_local = ints.shape[3]
    picked = jnp.take(occ_coeff, batch_ids, axis=0)
    batch_coeff = lax.all_gather(picked, "occ", axis=1, tiled=True)
    atom_total = batch_coeff.shape[1] // block_size
    left_all = batch_coeff.reshape(batch_size, atom_total, block_size)[:, blk_atoms[:, 0], :]
    vir_local = vir_coeff.shape[1]
    right_all = vir_coeff.reshape(atom_total, block_size, vir_local)[blk_atoms[:, 1]]
    live_count = blk_count[0]
    summed = half_transform(left_all, right_all, ints, live_count)
    group_count = lax.axis_size("aux")
    vir_group = vir_local // group_count
    fitted = summed.astype(jnp.bfloat16).reshape(batch_size, group_count, vir_group, aux_local)
    regrouped = lax.all_to_all(
        lax.all_to_all(fitted, "aux", split_axis=1, concat_axis=3, tiled=True),
        "occ",
        split_axis=3,
        concat_axis=2,
        tiled=True,
    )
    group_rows = regrouped[:, 0]
    group_width = group_rows.shape[1]
    flat_rows = group_rows.reshape(batch_size * group_width, group_rows.shape[2])
    kept_rows = lax.psum_scatter(
        jnp.einsum("icq,xq->cix", group_rows, flat_rows, preferred_element_type=jnp.float32),
        "occ",
        scatter_dimension=0,
        tiled=True,
    )
    pair_ints = jnp.transpose(
        kept_rows.reshape(vir_group, batch_size, batch_size, group_width), (1, 0, 2, 3)
    )[:, None]
    return pair_ints


def solution(mesh):
    in_specs = (
        P(None, None, None, "aux"),
        P("aux", None),
        P("aux"),
        P(None, "occ"),
        P(None, "occ"),
        P(),
    )
    out_specs = P(None, "aux", "occ", None, None)
    return jax.shard_map(
        on_device, mesh=mesh, in_specs=in_specs, out_specs=out_specs, check_vma=False
    )
```

profile of v0, /device:TPU:0, one launch (start us, length us, event | category | flops | bytes accessed | tf_op | source)
XLA Modules:
  0.0 128.6 jit_solution(15573331890887347236)
XLA Ops:
  0.0 0.0 copy-start
  0.0 0.8 compare_and_fusion
  0.8 0.8 compare_select_fusion.2
  2.3 0.8 fusion.14
  3.1 6.0 %gather_fusion = bf16[8,4096]{1,0:T(8,128)(2,1)S(1)} fusion(bf16[1280,4096]{1,0:T(8,128)(2,1)} %param.9, s32[1024]{0:T(1024)S(1)} %pad_clamp_fusion.2), kind=kCustom, calls=%fused_computation | custom fusion | bytes 131104 | tf_op jit(solution)/shard_map/jit(_take)/gather | solution.py:22
  9.0 1.2 gather.13
  10.2 0.0 copy-done
  10.2 0.6 gather_fusion.2
  10.9 2.2 %copy_select_fusion.1 = bf16[8,256,16]{2,0,1:T(8,128)(2,1)} fusion(bf16[8,256,16]{2,1,0:T(8,128)(2,1)} %gather.13, pred[8]{0:T(512)(128)(4,1)S(1)} %compare_and_fusion), kind=kLoop, calls=%fused_computation.13 | loop fusion | flops 32768 | bytes 131080 | tf_op jit(solution)/shard_map/jit(_take)/select_n | solution.py:22
  13.1 2.3 %gather_fusion.1 = bf16[32,8,16]{2,1,0:T(8,128)(2,1)} fusion(bf16[8,256,16]{2,0,1:T(8,128)(2,1)} %copy_select_fusion.1, s32[1024]{0:T(1024)S(1)} %get-tuple-element.8), kind=kCustom, calls=%fused_computation.1 | custom fusion | bytes 16512 | tf_op jit(solution)/shard_map/gather | solution.py:25
  15.3 8.2 %fusion.1 = bf16[32,8,16,512]{3,1,2,0:T(8,128)(2,1)S(1)} fusion(bf16[32,16,16,512]{3,2,1,0:T(8,128)(2,1)} %param.6, bf16[32,8,16]{2,1,0:T(8,128)(2,1)} %gather_fusion.1), kind=kOutput, calls=%fused_computation.5 | convolution fusion | flops 67108864 | bytes 12591104 | tf_op jit(solution)/shard_map/ikm,kmnq->kinq/dot_general | solution.py:8
  23.5 3.4 %fusion.7 = bf16[8,384,512]{2,1,0:T(8,128)(2,1)S(1)} fusion(bf16[32,8,16,512]{3,1,2,0:T(8,128)(2,1)S(1)} %fusion.1, pred[32]{0:T(512)(128)(4,1)S(1)} %iota_compare_fusion, bf16[32,16,384]{2,1,0:T(8,128)(2,1)S(1)} %gather_fusion.2), kind=kOutput, calls=%fused_computation.11 | convolution fusion | flops 1614282752 | bytes 7733280 | tf_op jit(solution)/shard_map/knv,kinq->ivq/dot_general | solution.py:15
  26.9 1.9 %copy.11 = bf16[8,384,512]{2,0,1:T(8,128)(2,1)S(1)} copy(bf16[8,384,512]{2,1,0:T(8,128)(2,1)S(1)} %fusion.7) | data formatting | bytes 6291456 | tf_op jit(solution)/shard_map/convert_element_type | solution.py:32
  28.9 78.3 %all_to_all.15 = bf16[8,32,12,512]{3,0,2,1:T(8,128)(2,1)S(1)} all-to-all(bf16[8,32,12,512]{3,0,2,1:T(8,128)(2,1)S(1)} %bitcast.44), channel_id=1, replica_groups=mesh['aux'=32,'occ'=1] {'aux'}, dimensions={1} | all-to-all | bytes 6291456 | tf_op jit(solution)/shard_map/all_to_all | solution.py:34
  107.2 3.4 %copy.12 = bf16[8,1,12,32,512]{4,3,2,0,1:T(8,128)(2,1)} copy(bf16[8,1,12,32,512]{4,0,2,3,1:T(8,128)(2,1)S(1)} %bitcast.45) | data formatting | bytes 6291456 | tf_op jit(solution)/shard_map/all_to_all | solution.py:34
  110.6 5.9 %reshape.58 = bf16[96,16384,1]{1,0,2:T(8,128)(2,1)} reshape(bf16[8,1,12,32,512]{4,3,2,0,1:T(8,128)(2,1)} %copy.12) | data formatting | bytes 6291456 | tf_op jit(solution)/shard_map/reshape;squeeze | solution.py:42
  116.5 5.4 %reshape.60 = bf16[8,12,16384]{2,1,0:T(8,128)(2,1)} reshape(bf16[8,1,12,32,512]{4,3,2,0,1:T(8,128)(2,1)} %copy.12) | data formatting | bytes 6291456 | tf_op jit(solution)/shard_map/squeeze | solution.py:40
  121.9 4.4 %convolution_bitcast_fusion = f32[12,8,96]{2,0,1:T(8,128)S(1)} fusion(bf16[96,16384,1]{1,0,2:T(8,128)(2,1)} %reshape.58, bf16[8,12,16384]{2,1,0:T(8,128)(2,1)} %reshape.60), kind=kOutput, calls=%fused_computation.12 | convolution fusion | flops 301989888 | bytes 6328320 | tf_op jit(solution)/shard_map/icq,xq->cix/dot_general | solution.py:44
  126.3 0.6 copy.15
  126.9 0.9 reshape.29
  127.9 0.8 copy.16
  (3 shorter events, 0.0 us)
Async XLA Ops:
  0.0 10.2 %copy-start = (bf16[4096,384]{1,0:T(8,128)(2,1)S(1)}, bf16[4096,384]{1,0:T(8,128)(2,1)}, u32[]{:S(2)}) copy-start(bf16[4096,384]{1,0:T(8,128)(2,1)} %param.10) | copy-start | bytes 9437188
where the time goes:
time: 129 us
  blocking collectives  78.3 us (61%)
  local copies, waits for them, and re-layouts  29.1 us (23%)
  matrix products  16 us (12%)
  other arithmetic  4.57 us (4%)
    all_to_all x1, blocking collectives, on_device(): lax.all_to_all(fitted, 'aux', split_axis=1, concat_axis=3, tiled=True)  78.3 us
    dot_general x1, matrix products, half_transform(): jnp.einsum('ikm,kmnq->kinq', left_rows, block_ints, preferred_element_typ...  8.21 us
    gather x2, local copies, waits for them, and re-layouts, on_device(): picked = jnp.take(occ_coeff, batch_ids, axis=0)  7.17 us
    another operation x1, local copies, waits for them, and re-layouts, on_device(): group_rows.reshape(batch_size * group_width, group_rows.shape[2])  5.89 us
    squeeze x1, local copies, waits for them, and re-layouts, on_device(): group_rows = regrouped[:, 0]  5.38 us
    dot_general x1, matrix products, on_device(): jnp.einsum('icq,xq->cix', group_rows, flat_rows, preferred_element_type=j...  4.38 us
    all_to_all x1, local copies, waits for them, and re-layouts, on_device(): lax.all_to_all(fitted, 'aux', split_axis=1, concat_axis=3, tiled=True)  3.43 us
    dot_general x1, matrix products, half_transform(): jnp.einsum('knv,kinq->ivq', right_rows, half_ints, preferred_element_type...  3.42 us

commit v1 on v0

--- a/solution.py
+++ b/solution.py
@@ -1,7 +1,249 @@
+import functools
+
 import jax
 import jax.numpy as jnp
 from jax import lax
+from jax.experimental import pallas as pl
+from jax.experimental.pallas import tpu as pltpu
 from jax.sharding import PartitionSpec as P
+
+LANES = 128
+ROWS = 16
+WINDOW = 3
+
+
+def partial_kernel(
+    group_width,
+    atoms_ref,
+    count_ref,
+    ids_ref,
+    ints_hbm,
+    occ_hbm,
+    vir_hbm,
+    out_ref,
+    ints_buf,
+    occ_buf,
+    vir_buf,
+    left_rows,
+    left_big,
+    right_rows,
+    right_t,
+    half_buf,
+    fit_buf,
+    ints_sem,
+    occ_sem,
+    vir_sem,
+):
+    slots, depth, aux_local = ints_buf.shape
+    batch = occ_buf.shape[0]
+    groups = fit_buf.shape[0]
+    virs = vir_buf.shape[1]
+    owners = lax.axis_size("aux")
+    me = lax.axis_index("aux")
+    atom_total = occ_hbm.shape[1] // ROWS
+    span = occ_hbm.shape[1] // owners
+    span_atoms = span // ROWS
+    window_atoms = WINDOW * span_atoms
+
+    copies = []
+    for i in range(batch):
+        base = pl.multiple_of((ids_ref[i] // ROWS) * ROWS, ROWS)
+        for b in range(WINDOW):
+            start = pl.multiple_of(lax.rem(me + b, owners) * span, LANES)
+            copies.append(
+                pltpu.make_async_copy(
+                    occ_hbm.at[pl.ds(base, ROWS), pl.ds(start, span)],
+                    occ_buf.at[i, :, pl.ds(b * span, span)],
+                    occ_sem.at[i, b],
+                )
+            )
+    for b in range(WINDOW):
+        start = pl.multiple_of(lax.rem(me + b, owners) * span, LANES)
+        copies.append(
+            pltpu.make_async_copy(
+                vir_hbm.at[pl.ds(start, span), :], vir_buf.at[pl.ds(b * span, span), :], vir_sem.at[b]
+            )
+        )
+    for copy in copies:
+        copy.start()
+    ints_copies = [
+        pltpu.make_async_copy(ints_hbm.at[k], ints_buf.at[k], ints_sem.at[k]) for k in range(slots)
+    ]
+    for copy in ints_copies:
+        copy.start()
+
+    def near(slot, side):
+        offset = atoms_ref[side, slot] - me * span_atoms
+        offset = jnp.where(offset < 0, offset + atom_total, offset)
+        return jnp.minimum(offset, window_atoms - 1)
+
+    wide = (groups * ROWS, virs)
+    row = lax.broadcasted_iota(jnp.int32, wide, 0)
+    col = lax.broadcasted_iota(jnp.int32, wide, 1)
+    keep = (row % ROWS < group_width) & (col == (row // ROWS) * group_width + row % ROWS)
+    spread = jnp.where(keep, 1.0, 0.0).astype(jnp.bfloat16)
+
+    tall = (window_atoms * batch, batch * ROWS)
+    row = lax.broadcasted_iota(jnp.int32, tall, 0) % batch
+    col = lax.broadcasted_iota(jnp.int32, tall, 1)
+    wanted = jnp.zeros(tall, jnp.int32)
+    for i in range(batch):
+        wanted = jnp.where(row == i, i * ROWS + ids_ref[i] % ROWS, wanted)
+    pick = jnp.where(col == wanted, 1.0, 0.0).astype(jnp.bfloat16)
+
+    shape = (window_atoms * ROWS, depth)
+    row = lax.broadcasted_iota(jnp.int32, shape, 0) % ROWS
+    col = lax.broadcasted_iota(jnp.int32, shape, 1) // ROWS
+    repeat = jnp.where(row == col, 1.0, 0.0).astype(jnp.bfloat16)
+
+    for copy in copies[: batch * WINDOW]:
+        copy.wait()
+    picked = jnp.dot(
+        pick, occ_buf[...].reshape(batch * ROWS, WINDOW * span), preferred_element_type=jnp.float32
+    )
+    row = lax.broadcasted_iota(jnp.int32, picked.shape, 0) // batch
+    col = lax.broadcasted_iota(jnp.int32, picked.shape, 1) // ROWS
+    picked = jnp.where(row == col, picked, 0.0).astype(jnp.bfloat16)
+    left_rows[...] = jnp.dot(picked, repeat, preferred_element_type=jnp.float32)
+
+    shape = (ROWS, depth)
+    diagonal = lax.broadcasted_iota(jnp.int32, shape, 0) == (
+        lax.broadcasted_iota(jnp.int32, shape, 1) % ROWS
+    )
+    for a in range(window_atoms):
+        rows = left_rows[a * batch : (a + 1) * batch, :]
+        for i in range(batch):
+            left_big[a, i * ROWS : (i + 1) * ROWS, :] = jnp.where(
+                diagonal, rows[i : i + 1, :], 0.0
+            ).astype(jnp.bfloat16)
+
+    for copy in copies[batch * WINDOW :]:
+        copy.wait()
+    for k in range(slots):
+        rows = vir_buf[pl.ds(pl.multiple_of(near(k, 1) * ROWS, ROWS), ROWS), :]
+        live = jnp.where(k < count_ref[0], 1.0, 0.0).astype(jnp.bfloat16)
+        right_rows[k * ROWS : (k + 1) * ROWS, :] = rows * live
+    right_t[...] = lax.dot_general(
+        spread, right_rows[...], (((1,), (1,)), ((), ())), preferred_element_type=jnp.float32
+    ).astype(jnp.bfloat16)
+
+    for k in range(slots):
+        ints_copies[k].wait()
+        half = jnp.dot(left_big[near(k, 0)], ints_buf[k], preferred_element_type=jnp.float32)
+        half = half.astype(jnp.bfloat16)
+        for i in range(batch):
+            half_buf[i, k * ROWS : (k + 1) * ROWS, :] = half[i * ROWS : (i + 1) * ROWS, :]
+
+    tile = 256
+    for i in range(batch):
+        for q in range(0, aux_local, tile):
+            fitted = jnp.dot(
+                right_t[...], half_buf[i, :, q : q + tile], preferred_element_type=jnp.float32
+            ).astype(jnp.bfloat16)
+            fit_buf[:, i * ROWS : (i + 1) * ROWS, q : q + tile] = fitted.reshape(groups, ROWS, tile)
+
+    upper = batch // 2 * ROWS
+    shape = (upper, LANES)
+    row = lax.broadcasted_iota(jnp.int32, shape, 0)
+    col = lax.broadcasted_iota(jnp.int32, shape, 1)
+    from_below = (col < upper) & (col > row)
+    top_half = lax.broadcasted_iota(jnp.int32, (8, LANES), 0) < 4
+    for g in range(groups):
+        gram = lax.dot_general(
+            fit_buf[g], fit_buf[g], (((1,), (1,)), ((), ())), preferred_element_type=jnp.float32
+        )
+        below = pltpu.roll(gram[upper:, :], upper + 1, 1)
+        packed = jnp.where(from_below, below, gram[:upper, :])
+        pieces = []
+        for i in range(0, batch // 2, 2):
+            first = packed[i * ROWS : (i + 1) * ROWS, :]
+            second = packed[(i + 1) * ROWS : (i + 2) * ROWS, :]
+            mixed = jnp.where(top_half, first[8:, :], pltpu.roll(second[8:, :], 4, 0))
+            pieces += [first[:8, :], mixed, second[:8, :]]
+        out_ref[g] = jnp.concatenate(pieces, axis=0).astype(jnp.bfloat16)
+
+
+def partial_sums(ints, blk_atoms, blk_count, occ_coeff, vir_coeff, batch_ids, groups):
+    slots, block, _, aux_local = ints.shape
+    batch = batch_ids.shape[0]
+    virs = vir_coeff.shape[1]
+    basis = occ_coeff.shape[1]
+    span = basis // groups
+    window_atoms = WINDOW * span // block
+    depth = block * block
+    group_width = virs // groups
+    smem = pl.BlockSpec(memory_space=pltpu.SMEM)
+    anywhere = pl.BlockSpec(memory_space=pltpu.HBM)
+    kept_rows = batch // 2 * group_width
+    return pl.pallas_call(
+        functools.partial(partial_kernel, group_width),
+        out_shape=jax.ShapeDtypeStruct((groups, kept_rows, LANES), jnp.bfloat16),
+        in_specs=[smem, smem, smem, anywhere, anywhere, anywhere],
+        out_specs=pl.BlockSpec(memory_space=pltpu.VMEM),
+        scratch_shapes=[
+            pltpu.VMEM((slots, depth, aux_local), jnp.bfloat16),
+            pltpu.VMEM((batch, ROWS, WINDOW * span), jnp.bfloat16),
+            pltpu.VMEM((WINDOW * span, virs), jnp.bfloat16),
+            pltpu.VMEM((window_atoms * batch, depth), jnp.float32),
+            pltpu.VMEM((window_atoms, batch * ROWS, depth), jnp.bfloat16),
+            pltpu.VMEM((slots * ROWS, virs), jnp.bfloat16),
+            pltpu.VMEM((groups * ROWS, slots * ROWS), jnp.bfloat16),
+            pltpu.VMEM((batch, slots * ROWS, aux_local), jnp.bfloat16),
+            pltpu.VMEM((groups, batch * ROWS, aux_local), jnp.bfloat16),
+            pltpu.SemaphoreType.DMA((slots,)),
+            pltpu.SemaphoreType.DMA((batch, WINDOW)),
+            pltpu.SemaphoreType.DMA((WINDOW,)),
+        ],
+        compiler_params=pltpu.CompilerParams(vmem_limit_bytes=40 * 1024 * 1024),
+    )(
+        blk_atoms.T,
+        blk_count,
+        batch_ids,
+        ints.reshape(slots, depth, aux_local),
+        occ_coeff,
+        vir_coeff,
+    )
+
+
+def total_kernel(group_width, batch, parts_ref, out_ref):
+    total = jnp.sum(parts_ref[...].astype(jnp.float32), axis=0)
+    upper = batch // 2 * ROWS
+    top_half = lax.broadcasted_iota(jnp.int32, (8, LANES), 0) < 4
+    pieces = []
+    for i in range(0, batch // 2, 2):
+        first, mixed, second = (
+            total[(3 * (i // 2) + s) * 8 : (3 * (i // 2) + s + 1) * 8, :] for s in range(3)
+        )
+        pieces += [
+            first,
+            jnp.where(top_half, mixed, 0.0),
+            second,
+            jnp.where(top_half, pltpu.roll(mixed, 4, 0), 0.0),
+        ]
+    above = jnp.concatenate(pieces, axis=0)
+    both = jnp.concatenate([above, pltpu.roll(above, upper - 1, 1)], axis=0)
+    shape = (2 * upper, 2 * upper)
+    row = lax.broadcasted_iota(jnp.int32, shape, 0)
+    col = lax.broadcasted_iota(jnp.int32, shape, 1)
+    direct = ((row < upper) & ((col >= upper) | (col <= row))) | ((row >= upper) & (col >= row))
+    whole = jnp.where(direct, both, both.T)
+    for i in range(batch):
+        for c in range(0, group_width, 8):
+            rows = whole[i * ROWS + c : i * ROWS + c + 8, :]
+            count = min(8, group_width - c)
+            for j in range(batch):
+                moved = rows if j == 0 else pltpu.roll(rows, LANES - j * ROWS, 1)
+                start = (i * group_width + c) * batch + j
+                out_ref[pl.ds(start, count, stride=batch), :] = moved[:count, :group_width]
+
+
+def total_sums(parts, batch, group_width):
+    return pl.pallas_call(
+        functools.partial(total_kernel, group_width, batch),
+        out_shape=jax.ShapeDtypeStruct((batch * group_width * batch, group_width), jnp.float32),
+        in_specs=[pl.BlockSpec(memory_space=pltpu.VMEM)],
+        out_specs=pl.BlockSpec(memory_space=pltpu.VMEM),
+    )(parts)
 
 
 def half_transform(left_rows, right_rows, block_ints, live_count):
@@ -15,7 +257,7 @@
     return jnp.einsum("knv,kinq->ivq", right_rows, half_ints, preferred_element_type=jnp.float32)
 
 
-def on_device(ints, blk_atoms, blk_count, occ_coeff, vir_coeff, batch_ids):
+def regrouping_device(ints, blk_atoms, blk_count, occ_coeff, vir_coeff, batch_ids):
     batch_size = batch_ids.shape[0]
     block_size = ints.shape[1]
     aux_local = ints.shape[3]
@@ -52,6 +294,18 @@
     return pair_ints
 
 
+def on_device(ints, blk_atoms, blk_count, occ_coeff, vir_coeff, batch_ids):
+    if lax.axis_size("occ") > 1:
+        return regrouping_device(ints, blk_atoms, blk_count, occ_coeff, vir_coeff, batch_ids)
+    batch = batch_ids.shape[0]
+    groups = lax.axis_size("aux")
+    group_width = vir_coeff.shape[1] // groups
+    parts = partial_sums(ints, blk_atoms, blk_count, occ_coeff, vir_coeff, batch_ids, groups)
+    parts = lax.all_to_all(parts, "aux", split_axis=0, concat_axis=0, tiled=True)
+    total = total_sums(parts, batch, group_width)
+    return total.reshape(batch, 1, group_width, batch, group_width)
+
+
 def solution(mesh):
     in_specs = (
         P(None, None, None, "aux"),

time: 129 us -> 43.2 us (0.33)
  blocking collectives: 78.3 us -> 20.4 us
  local copies, waits for them, and re-layouts: 29.1 us -> 6.6 us
  matrix products: 16 us -> 0 us
  Pallas kernels: 0 us -> 15.3 us
  other arithmetic: 4.57 us -> 0 us
    all_to_all x1, blocking collectives: 78.3 us -> 20.4 us  [on_device(): lax.all_to_all(parts, 'aux', split_axis=0, concat_axis=0, tiled=True)]
    dot_general x3 -> x0, matrix products: 16 us -> none  [the longest x1 8.21 us: half_transform(): jnp.einsum('ikm,kmnq->kinq', left_rows, block_ints, preferred_element_typ...]
    pallas_call x0 -> x2, Pallas kernels: none -> 15.3 us  [the longest x1 13.1 us: partial_sums(): pl.pallas_call(functools.partial(partial_kernel, group_width), out_shape=...]
    gather x4 -> x0, local copies, waits for them, and re-layouts: 10.1 us -> none  [the longest x2 7.17 us: on_device(): picked = jnp.take(occ_coeff, batch_ids, axis=0)]
    unnamed x2 -> x8, local copies, waits for them, and re-layouts: 0.01 us -> 6.6 us
    another operation x1 -> x0, local copies, waits for them, and re-layouts: 5.89 us -> none  [on_device(): group_rows.reshape(batch_size * group_width, group_rows.shape[2])]
    squeeze x1 -> x0, local copies, waits for them, and re-layouts: 5.38 us -> none  [on_device(): group_rows = regrouped[:, 0]]
    select_n x3 -> x0, other arithmetic: 3.74 us -> none  [the longest x2 2.98 us: on_device(): picked = jnp.take(occ_coeff, batch_ids, axis=0)]
where the time goes in v1:
time: 43.2 us; the launch traced here: 42.9 us
  blocking collectives  20.4 us (47%)
  Pallas kernels  15.3 us (35%)
  local copies, waits for them, and re-layouts  6.6 us (15%)
  between operations  0.67 us (2%)
    all_to_all x1, blocking collectives, on_device(): lax.all_to_all(parts, 'aux', split_axis=0, concat_axis=0, tiled=True)  20.4 us
    pallas_call x1, Pallas kernels, partial_sums(): pl.pallas_call(functools.partial(partial_kernel, group_width), out_shape=...  13.1 us
    unnamed x8, local copies, waits for them, and re-layouts  6.6 us
    pallas_call x1, Pallas kernels, total_sums(): pl.pallas_call(functools.partial(total_kernel, group_width, batch), out_s...  2.14 us

profile of v1, /device:TPU:0, one launch (start us, length us, event | category | flops | bytes accessed | tf_op | source)
XLA Modules:
  0.0 42.9 jit_solution(9609939350269009834)
XLA Ops:
  0.7 0.0 copy-start
  0.7 3.4 %copy-done = bf16[32,16,16,512]{3,2,1,0:T(8,128)(2,1)S(1)} copy-done((bf16[32,16,16,512]{3,2,1,0:T(8,128)(2,1)S(1)}, bf16[32,16,16,512]{3,2,1,0:T(8,128)(2,1)}, u32[]{:S(2)}) %copy-start) | copy-done | bytes 8388632
  4.0 0.0 copy-start.1
  4.0 1.9 %copy-done.1 = bf16[4096,384]{1,0:T(8,128)(2,1)S(1)} copy-done((bf16[4096,384]{1,0:T(8,128)(2,1)S(1)}, bf16[4096,384]{1,0:T(8,128)(2,1)}, u32[]{:S(2)}) %copy-start.1) | copy-done | bytes 3145752
  5.9 0.0 copy-start.2
  5.9 0.7 %copy-done.2 = s32[32,2]{0,1:T(2,128)S(1)} copy-done((s32[32,2]{0,1:T(2,128)S(1)}, s32[32,2]{0,1:T(2,128)}, u32[]{:S(2)}) %copy-start.2) | copy-done | bytes 280
  6.6 0.0 copy-start.3
  6.6 0.7 %copy-done.3 = s32[8]{0:T(128)S(1)} copy-done((s32[8]{0:T(128)S(1)}, s32[8]{0:T(128)}, u32[]{:S(2)}) %copy-start.3) | copy-done | bytes 56
  7.3 13.1 %shard_map.64 = bf16[32,48,128]{2,1,0:T(8,128)(2,1)S(1)} custom-call(s32[2,32]{1,0:T(2,128)S(1)} %bitcast.6, s32[1]{0:T(128)S(6)} %copy.8.count_ref, s32[8]{0:T(128)S(1)} %copy-done.3, bf16[32,256,512]{2,1,0:T(8,128)(2,1)S(1)} %bitcast.5, bf16[1280,4096]{1,0:T(8,128)(2,1)} %occ_hbm.1, bf16[4096,384]{1,0:T(8,128)(2,1)S(1)} %copy-done.1), custom_call_target="tpu_custom_call" | custom-call | tf_op jit(solution)/shard_map/pallas_call | solution.py:178
  20.4 20.4 %all_to_all.5.parts_ref = bf16[32,48,128]{2,1,0:T(8,128)(2,1)} all-to-all(bf16[32,48,128]{2,1,0:T(8,128)(2,1)S(1)} %shard_map.64), channel_id=1, replica_groups=mesh['aux'=32,'occ'=1] {'aux'}, dimensions={0} | all-to-all | bytes 786432 | tf_op jit(solution)/shard_map/all_to_all | solution.py:304
  40.8 2.1 %shard_map.65 = f32[768,12]{1,0:T(8,128)} custom-call(bf16[32,48,128]{2,1,0:T(8,128)(2,1)} %all_to_all.5.parts_ref), custom_call_target="tpu_custom_call" | custom-call | tf_op jit(solution)/shard_map/pallas_call | solution.py:241
Async XLA Ops:
  0.7 3.4 %copy-start = (bf16[32,16,16,512]{3,2,1,0:T(8,128)(2,1)S(1)}, bf16[32,16,16,512]{3,2,1,0:T(8,128)(2,1)}, u32[]{:S(2)}) copy-start(bf16[32,16,16,512]{3,2,1,0:T(8,128)(2,1)} %param.6) | copy-start | bytes 25165828
  4.0 1.9 %copy-start.1 = (bf16[4096,384]{1,0:T(8,128)(2,1)S(1)}, bf16[4096,384]{1,0:T(8,128)(2,1)}, u32[]{:S(2)}) copy-start(bf16[4096,384]{1,0:T(8,128)(2,1)} %vir_hbm.1) | copy-start | bytes 9437188
  5.9 0.7 %copy-start.2 = (s32[32,2]{0,1:T(2,128)S(1)}, s32[32,2]{0,1:T(2,128)}, u32[]{:S(2)}) copy-start(s32[32,2]{0,1:T(2,128)} %param.7) | copy-start | bytes 772
  6.6 0.7 %copy-start.3 = (s32[8]{0:T(128)S(1)}, s32[8]{0:T(128)}, u32[]{:S(2)}) copy-start(s32[8]{0:T(128)} %ids_ref.1) | copy-start | bytes 100

commit v2 on v1

--- a/solution.py
+++ b/solution.py
@@ -10,17 +10,26 @@
 LANES = 128
 ROWS = 16
 WINDOW = 3
+CHUNKS = 1
+PARTS = 2
+EARLY = 1
+PRIO = 1
+TILE = 256
 
 
 def partial_kernel(
     group_width,
+    atoms_hbm,
+    count_hbm,
+    ids_hbm,
+    ints_hbm,
+    occ_hbm,
+    vir_hbm,
+    keep_ref,
+    send_ref,
     atoms_ref,
     count_ref,
     ids_ref,
-    ints_hbm,
-    occ_hbm,
-    vir_hbm,
-    out_ref,
     ints_buf,
     occ_buf,
     vir_buf,
@@ -30,6 +39,7 @@
     right_t,
     half_buf,
     fit_buf,
+    small_sem,
     ints_sem,
     occ_sem,
     vir_sem,
@@ -43,81 +53,83 @@
     atom_total = occ_hbm.shape[1] // ROWS
     span = occ_hbm.shape[1] // owners
     span_atoms = span // ROWS
-    window_atoms = WINDOW * span_atoms
-
-    copies = []
+    window_atoms = left_big.shape[0]
+    step = slots // CHUNKS
+    part = aux_local // PARTS
+
+    small_copies = [
+        pltpu.make_async_copy(source, target, small_sem.at[s])
+        for s, (source, target) in enumerate(
+            ((ids_hbm, ids_ref), (atoms_hbm, atoms_ref), (count_hbm, count_ref))
+        )
+    ]
+    for copy in small_copies:
+        copy.start()
+    starts = [pl.multiple_of(lax.rem(me + b, owners) * span, LANES) for b in range(WINDOW)]
+    vir_copies = [
+        pltpu.make_async_copy(
+            vir_hbm.at[pl.ds(starts[b], span), :], vir_buf.at[pl.ds(b * span, span), :], vir_sem.at[b]
+        )
+        for b in range(WINDOW)
+    ]
+    for copy in vir_copies:
+        copy.start()
+    ints_copies = []
+    for p in range(PARTS):
+        for c in range(CHUNKS):
+            block = (pl.ds(c * step, step), slice(None), pl.ds(p * part, part))
+            ints_copies.append(
+                pltpu.make_async_copy(ints_hbm.at[block], ints_buf.at[block], ints_sem.at[p, c])
+            )
+    for copy in ints_copies[:EARLY]:
+        copy.start(priority=PRIO)
+    small_copies[0].wait()
+    occ_copies = []
     for i in range(batch):
-        base = pl.multiple_of((ids_ref[i] // ROWS) * ROWS, ROWS)
+        base = pl.multiple_of(ids_ref[i] & -ROWS, ROWS)
         for b in range(WINDOW):
-            start = pl.multiple_of(lax.rem(me + b, owners) * span, LANES)
-            copies.append(
+            occ_copies.append(
                 pltpu.make_async_copy(
-                    occ_hbm.at[pl.ds(base, ROWS), pl.ds(start, span)],
+                    occ_hbm.at[pl.ds(base, ROWS), pl.ds(starts[b], span)],
                     occ_buf.at[i, :, pl.ds(b * span, span)],
                     occ_sem.at[i, b],
                 )
             )
-    for b in range(WINDOW):
-        start = pl.multiple_of(lax.rem(me + b, owners) * span, LANES)
-        copies.append(
-            pltpu.make_async_copy(
-                vir_hbm.at[pl.ds(start, span), :], vir_buf.at[pl.ds(b * span, span), :], vir_sem.at[b]
-            )
-        )
-    for copy in copies:
+    for copy in occ_copies:
         copy.start()
-    ints_copies = [
-        pltpu.make_async_copy(ints_hbm.at[k], ints_buf.at[k], ints_sem.at[k]) for k in range(slots)
-    ]
-    for copy in ints_copies:
-        copy.start()
+    for copy in ints_copies[EARLY:]:
+        copy.start(priority=PRIO)
+    for copy in small_copies[1:]:
+        copy.wait()
 
     def near(slot, side):
         offset = atoms_ref[side, slot] - me * span_atoms
         offset = jnp.where(offset < 0, offset + atom_total, offset)
         return jnp.minimum(offset, window_atoms - 1)
 
+    row_bits = ROWS.bit_length() - 1
+    batch_bits = batch.bit_length() - 1
     wide = (groups * ROWS, virs)
     row = lax.broadcasted_iota(jnp.int32, wide, 0)
     col = lax.broadcasted_iota(jnp.int32, wide, 1)
-    keep = (row % ROWS < group_width) & (col == (row // ROWS) * group_width + row % ROWS)
-    spread = jnp.where(keep, 1.0, 0.0).astype(jnp.bfloat16)
-
-    tall = (window_atoms * batch, batch * ROWS)
-    row = lax.broadcasted_iota(jnp.int32, tall, 0) % batch
+    inner = row & (ROWS - 1)
+    target = jnp.where(inner < group_width, (row >> row_bits) * group_width + inner, -1)
+    spread = jnp.where(col == target, 1.0, 0.0).astype(jnp.bfloat16)
+
+    shape = (WINDOW * span, depth)
+    row = lax.broadcasted_iota(jnp.int32, shape, 0) & (ROWS - 1)
+    col = lax.broadcasted_iota(jnp.int32, shape, 1) >> row_bits
+    repeat = jnp.where(row == col, 1.0, 0.0).astype(jnp.bfloat16)
+
+    tall = (batch, batch * ROWS)
+    row = lax.broadcasted_iota(jnp.int32, tall, 0)
     col = lax.broadcasted_iota(jnp.int32, tall, 1)
     wanted = jnp.zeros(tall, jnp.int32)
     for i in range(batch):
-        wanted = jnp.where(row == i, i * ROWS + ids_ref[i] % ROWS, wanted)
+        wanted = jnp.where(row == i, i * ROWS + (ids_ref[i] & (ROWS - 1)), wanted)
     pick = jnp.where(col == wanted, 1.0, 0.0).astype(jnp.bfloat16)
 
-    shape = (window_atoms * ROWS, depth)
-    row = lax.broadcasted_iota(jnp.int32, shape, 0) % ROWS
-    col = lax.broadcasted_iota(jnp.int32, shape, 1) // ROWS
-    repeat = jnp.where(row == col, 1.0, 0.0).astype(jnp.bfloat16)
-
-    for copy in copies[: batch * WINDOW]:
-        copy.wait()
-    picked = jnp.dot(
-        pick, occ_buf[...].reshape(batch * ROWS, WINDOW * span), preferred_element_type=jnp.float32
-    )
-    row = lax.broadcasted_iota(jnp.int32, picked.shape, 0) // batch
-    col = lax.broadcasted_iota(jnp.int32, picked.shape, 1) // ROWS
-    picked = jnp.where(row == col, picked, 0.0).astype(jnp.bfloat16)
-    left_rows[...] = jnp.dot(picked, repeat, preferred_element_type=jnp.float32)
-
-    shape = (ROWS, depth)
-    diagonal = lax.broadcasted_iota(jnp.int32, shape, 0) == (
-        lax.broadcasted_iota(jnp.int32, shape, 1) % ROWS
-    )
-    for a in range(window_atoms):
-        rows = left_rows[a * batch : (a + 1) * batch, :]
-        for i in range(batch):
-            left_big[a, i * ROWS : (i + 1) * ROWS, :] = jnp.where(
-                diagonal, rows[i : i + 1, :], 0.0
-            ).astype(jnp.bfloat16)
-
-    for copy in copies[batch * WINDOW :]:
+    for copy in vir_copies:
         copy.wait()
     for k in range(slots):
         rows = vir_buf[pl.ds(pl.multiple_of(near(k, 1) * ROWS, ROWS), ROWS), :]
@@ -127,20 +139,46 @@
         spread, right_rows[...], (((1,), (1,)), ((), ())), preferred_element_type=jnp.float32
     ).astype(jnp.bfloat16)
 
-    for k in range(slots):
-        ints_copies[k].wait()
-        half = jnp.dot(left_big[near(k, 0)], ints_buf[k], preferred_element_type=jnp.float32)
-        half = half.astype(jnp.bfloat16)
+    for copy in occ_copies:
+        copy.wait()
+    picked = jnp.dot(
+        pick, occ_buf[...].reshape(batch * ROWS, WINDOW * span), preferred_element_type=jnp.float32
+    )
+    picked = jnp.concatenate([picked] * window_atoms, axis=0)
+    row = lax.broadcasted_iota(jnp.int32, picked.shape, 0) >> batch_bits
+    col = lax.broadcasted_iota(jnp.int32, picked.shape, 1) >> row_bits
+    picked = jnp.where(row == col, picked, 0.0).astype(jnp.bfloat16)
+    left_rows[...] = jnp.dot(picked, repeat, preferred_element_type=jnp.float32)
+
+    shape = (ROWS, depth)
+    diagonal = lax.broadcasted_iota(jnp.int32, shape, 0) == (
+        lax.broadcasted_iota(jnp.int32, shape, 1) & (ROWS - 1)
+    )
+    for a in range(window_atoms):
+        rows = left_rows[a * batch : (a + 1) * batch, :]
         for i in range(batch):
-            half_buf[i, k * ROWS : (k + 1) * ROWS, :] = half[i * ROWS : (i + 1) * ROWS, :]
-
-    tile = 256
-    for i in range(batch):
-        for q in range(0, aux_local, tile):
-            fitted = jnp.dot(
-                right_t[...], half_buf[i, :, q : q + tile], preferred_element_type=jnp.float32
+            left_big[a, i * ROWS : (i + 1) * ROWS, :] = jnp.where(
+                diagonal, rows[i : i + 1, :], 0.0
             ).astype(jnp.bfloat16)
-            fit_buf[:, i * ROWS : (i + 1) * ROWS, q : q + tile] = fitted.reshape(groups, ROWS, tile)
+
+    for p in range(PARTS):
+        cols = slice(p * part, (p + 1) * part)
+        for c in range(CHUNKS):
+            ints_copies[p * CHUNKS + c].wait()
+            for k in range(c * step, (c + 1) * step):
+                half = jnp.dot(
+                    left_big[near(k, 0)], ints_buf[k, :, cols], preferred_element_type=jnp.float32
+                ).astype(jnp.bfloat16)
+                for i in range(batch):
+                    half_buf[i, k * ROWS : (k + 1) * ROWS, cols] = half[i * ROWS : (i + 1) * ROWS, :]
+        for i in range(batch):
+            for q in range(p * part, (p + 1) * part, TILE):
+                fitted = jnp.dot(
+                    right_t[...], half_buf[i, :, q : q + TILE], preferred_element_type=jnp.float32
+                ).astype(jnp.bfloat16)
+                fit_buf[:, i * ROWS : (i + 1) * ROWS, q : q + TILE] = fitted.reshape(
+                    groups, ROWS, TILE
+                )
 
     upper = batch // 2 * ROWS
     shape = (upper, LANES)
@@ -148,19 +186,25 @@
     col = lax.broadcasted_iota(jnp.int32, shape, 1)
     from_below = (col < upper) & (col > row)
     top_half = lax.broadcasted_iota(jnp.int32, (8, LANES), 0) < 4
-    for g in range(groups):
-        gram = lax.dot_general(
-            fit_buf[g], fit_buf[g], (((1,), (1,)), ((), ())), preferred_element_type=jnp.float32
+    own = lax.rem(me, 2)
+    high = batch * ROWS
+    for first_group in range(0, groups, 2):
+        both = fit_buf[first_group : first_group + 2].reshape(2 * high, aux_local)
+        grams = lax.dot_general(
+            both, both, (((1,), (1,)), ((), ())), preferred_element_type=jnp.float32
         )
-        below = pltpu.roll(gram[upper:, :], upper + 1, 1)
-        packed = jnp.where(from_below, below, gram[:upper, :])
-        pieces = []
-        for i in range(0, batch // 2, 2):
-            first = packed[i * ROWS : (i + 1) * ROWS, :]
-            second = packed[(i + 1) * ROWS : (i + 2) * ROWS, :]
-            mixed = jnp.where(top_half, first[8:, :], pltpu.roll(second[8:, :], 4, 0))
-            pieces += [first[:8, :], mixed, second[:8, :]]
-        out_ref[g] = jnp.concatenate(pieces, axis=0).astype(jnp.bfloat16)
+        for g in range(2):
+            gram = grams[g * high : (g + 1) * high, g * high : (g + 1) * high]
+            below = pltpu.roll(gram[upper:, :], upper + 1, 1)
+            packed = jnp.where(from_below, below, gram[:upper, :])
+            halves = []
+            for i in range(0, batch // 2, 2):
+                first = packed[i * ROWS : (i + 1) * ROWS, :]
+                second = packed[(i + 1) * ROWS : (i + 2) * ROWS, :]
+                mixed = jnp.where(top_half, first[8:, :], pltpu.roll(second[8:, :], 4, 0))
+                halves.append(jnp.concatenate([first[:8, :], mixed, second[:8, :]], axis=0))
+            keep_ref[first_group + g] = jnp.where(own == 0, halves[0], halves[1])
+            send_ref[first_group + g] = jnp.where(own == 0, halves[1], halves[0])
 
 
 def partial_sums(ints, blk_atoms, blk_count, occ_coeff, vir_coeff, batch_ids, groups):
@@ -169,18 +213,20 @@
     virs = vir_coeff.shape[1]
     basis = occ_coeff.shape[1]
     span = basis // groups
-    window_atoms = WINDOW * span // block
+    window_atoms = (WINDOW - 1) * span // block + 1
     depth = block * block
     group_width = virs // groups
-    smem = pl.BlockSpec(memory_space=pltpu.SMEM)
-    anywhere = pl.BlockSpec(memory_space=pltpu.HBM)
-    kept_rows = batch // 2 * group_width
+    far = pl.BlockSpec(memory_space=pltpu.HBM)
+    result = jax.ShapeDtypeStruct((groups, batch // 4 * group_width, LANES), jnp.float32)
     return pl.pallas_call(
         functools.partial(partial_kernel, group_width),
-        out_shape=jax.ShapeDtypeStruct((groups, kept_rows, LANES), jnp.bfloat16),
-        in_specs=[smem, smem, smem, anywhere, anywhere, anywhere],
-        out_specs=pl.BlockSpec(memory_space=pltpu.VMEM),
+        out_shape=(result, result),
+        in_specs=[far] * 6,
+        out_specs=[pl.BlockSpec(memory_space=pltpu.VMEM)] * 2,
         scratch_shapes=[
+            pltpu.SMEM((2, slots), jnp.int32),
+            pltpu.SMEM((1,), jnp.int32),
+            pltpu.SMEM((batch,), jnp.int32),
             pltpu.VMEM((slots, depth, aux_local), jnp.bfloat16),
             pltpu.VMEM((batch, ROWS, WINDOW * span), jnp.bfloat16),
             pltpu.VMEM((WINDOW * span, virs), jnp.bfloat16),
@@ -190,11 +236,12 @@
             pltpu.VMEM((groups * ROWS, slots * ROWS), jnp.bfloat16),
             pltpu.VMEM((batch, slots * ROWS, aux_local), jnp.bfloat16),
             pltpu.VMEM((groups, batch * ROWS, aux_local), jnp.bfloat16),
-            pltpu.SemaphoreType.DMA((slots,)),
+            pltpu.SemaphoreType.DMA((3,)),
+            pltpu.SemaphoreType.DMA((PARTS, CHUNKS)),
             pltpu.SemaphoreType.DMA((batch, WINDOW)),
             pltpu.SemaphoreType.DMA((WINDOW,)),
         ],
-        compiler_params=pltpu.CompilerParams(vmem_limit_bytes=40 * 1024 * 1024),
+        compiler_params=pltpu.CompilerParams(vmem_limit_bytes=63 * 1024 * 1024),
     )(
         blk_atoms.T,
         blk_count,
@@ -206,7 +253,10 @@
 
 
 def total_kernel(group_width, batch, parts_ref, out_ref):
-    total = jnp.sum(parts_ref[...].astype(jnp.float32), axis=0)
+    owners, rows, _ = parts_ref.shape
+    total = jnp.sum(
+        parts_ref[...].astype(jnp.float32).reshape(owners // 2, 2 * rows, LANES), axis=0
+    )
     upper = batch // 2 * ROWS
     top_half = lax.broadcasted_iota(jnp.int32, (8, LANES), 0) < 4
     pieces = []
@@ -300,7 +350,9 @@
     batch = batch_ids.shape[0]
     groups = lax.axis_size("aux")
     group_width = vir_coeff.shape[1] // groups
-    parts = partial_sums(ints, blk_atoms, blk_count, occ_coeff, vir_coeff, batch_ids, groups)
+    keep, send = partial_sums(ints, blk_atoms, blk_count, occ_coeff, vir_coeff, batch_ids, groups)
+    partners = [(owner, owner ^ 1) for owner in range(groups)]
+    parts = (keep + lax.ppermute(send, "aux", partners)).astype(jnp.bfloat16)
     parts = lax.all_to_all(parts, "aux", split_axis=0, concat_axis=0, tiled=True)
     total = total_sums(parts, batch, group_width)
     return total.reshape(batch, 1, group_width, batch, group_width)

time: 43.2 us -> 30.7 us (0.71)
  local copies, waits for them, and re-layouts: 6.6 us -> 0 us
  Pallas kernels: 15.3 us -> 10.6 us
  blocking collectives: 20.4 us -> 16 us
  waiting for transfers between devices: 0 us -> 1.56 us
  other arithmetic: 0 us -> 1.04 us
  starting transfers between devices: 0 us -> 0.52 us
    unnamed x8 -> x0, local copies, waits for them, and re-layouts: 6.6 us -> none
    pallas_call x1, Pallas kernels: 13.1 us -> 8.51 us  [partial_sums(): pl.pallas_call(functools.partial(partial_kernel, group_width), out_shape=...]
    all_to_all x1, blocking collectives: 20.4 us -> 16 us  [on_device(): lax.all_to_all(parts, 'aux', split_axis=0, concat_axis=0, tiled=True)]
    ppermute x0 -> x1, waiting for transfers between devices: none -> 1.56 us  [on_device(): parts = (keep + lax.ppermute(send, 'aux', partners)).astype(jnp.bfloat16)]
    convert_element_type x0 -> x1, other arithmetic: none -> 1.04 us  [on_device(): parts = (keep + lax.ppermute(send, 'aux', partners)).astype(jnp.bfloat16)]
    ppermute x0 -> x1, starting transfers between devices: none -> 0.52 us  [on_device(): parts = (keep + lax.ppermute(send, 'aux', partners)).astype(jnp.bfloat16)]
  transfers between devices with their start and end apart: 0 -> 1, of which waited for: 0 -> 1; matrix products, arithmetic and copies ran while one was open for 0% -> 0% of each run, Pallas kernels for 0% -> 0%
where the time goes in v2:
time: 30.7 us; the launch traced here: 30.3 us
  blocking collectives  16 us (52%)
  Pallas kernels  10.6 us (35%)
  waiting for transfers between devices  1.56 us (5%)
  other arithmetic  1.04 us (3%)
  between operations  0.66 us (2%)
  starting transfers between devices  0.52 us (2%)
    all_to_all x1, blocking collectives, on_device(): lax.all_to_all(parts, 'aux', split_axis=0, concat_axis=0, tiled=True)  16 us
    pallas_call x1, Pallas kernels, partial_sums(): pl.pallas_call(functools.partial(partial_kernel, group_width), out_shape=...  8.51 us
    pallas_call x1, Pallas kernels, total_sums(): pl.pallas_call(functools.partial(total_kernel, group_width, batch), out_s...  2.04 us
    ppermute x1, waiting for transfers between devices, on_device(): parts = (keep + lax.ppermute(send, 'aux', partners)).astype(jnp.bfloat16)  1.56 us
    convert_element_type x1, other arithmetic, on_device(): parts = (keep + lax.ppermute(send, 'aux', partners)).astype(jnp.bfloat16)  1.04 us
  transfers between devices with their start and end apart: 1, of which 1 were waited for; matrix products, arithmetic and copies ran while one was open for 0% of the time, Pallas kernels for 0%

profile of v2, /device:TPU:0, one launch (start us, length us, event | category | flops | bytes accessed | tf_op | source)
XLA Modules:
  0.0 30.3 jit_solution(16530172618707259422)
XLA Ops:
  0.7 8.5 %shard_map.64 = (f32[32,24,128]{2,1,0:T(8,128)}, f32[32,24,128]{2,1,0:T(8,128)}) custom-call(s32[2,32]{1,0:T(2,128)} %bitcast.6, s32[1]{0:T(128)S(6)} %copy.8.count_hbm, s32[8]{0:T(128)} %ids_hbm.1, bf16[32,256,512]{2,1,0:T(8,128)(2,1)} %bitcast.5, bf16[1280,4096]{1,0:T(8,128)(2,1)} %occ_hbm.1, bf16[4096,384]{1,0:T(8,128)(2,1)} %vir_hbm.1), custom_call_target="tpu_custom_call" | custom-call | tf_op jit(solution)/shard_map/pallas_call | solution.py:221
  9.2 0.5 %collective-permute-start = (f32[32,24,128]{2,1,0:T(8,128)}, f32[32,24,128]{2,1,0:T(8,128)S(1)}, u32[]{:S(2)}, u32[]{:S(2)}) collective-permute-start(f32[32,24,128]{2,1,0:T(8,128)} %get-tuple-element.8), channel_id=1, source_target_pairs={{0,1},{1,0},{2,3},{3,2},{4,5},{5,4},{6,7},{7,6},{8,9},{9,8},{10,11... | collective-permute-start | bytes 1179656 | tf_op jit(solution)/shard_map/ppermute | solution.py:355
  9.7 1.6 %collective-permute-done = f32[32,24,128]{2,1,0:T(8,128)S(1)} collective-permute-done((f32[32,24,128]{2,1,0:T(8,128)}, f32[32,24,128]{2,1,0:T(8,128)S(1)}, u32[]{:S(2)}, u32[]{:S(2)}) %collective-permute-start) | collective-permute-done | bytes 393248 | tf_op jit(solution)/shard_map/ppermute | solution.py:355
  11.3 1.0 %add_convert_fusion = bf16[32,24,128]{2,1,0:T(8,128)(2,1)S(1)} fusion(f32[32,24,128]{2,1,0:T(8,128)} %get-tuple-element.7, f32[32,24,128]{2,1,0:T(8,128)S(1)} %collective-permute-done), kind=kLoop, calls=%fused_computation | loop fusion | flops 196608 | bytes 983040 | tf_op jit(solution)/shard_map/convert_element_type | solution.py:355
  12.3 16.0 %all_to_all.5.parts_ref = bf16[32,24,128]{2,1,0:T(8,128)(2,1)} all-to-all(bf16[32,24,128]{2,1,0:T(8,128)(2,1)S(1)} %add_convert_fusion), channel_id=1, replica_groups=mesh['aux'=32,'occ'=1] {'aux'}, dimensions={0} | all-to-all | bytes 393216 | tf_op jit(solution)/shard_map/all_to_all | solution.py:356
  28.3 2.0 %shard_map.65 = f32[768,12]{1,0:T(8,128)} custom-call(bf16[32,24,128]{2,1,0:T(8,128)(2,1)} %all_to_all.5.parts_ref), custom_call_target="tpu_custom_call" | custom-call | tf_op jit(solution)/shard_map/pallas_call | solution.py:291
Async XLA Ops:
  9.2 2.1 %collective-permute-start = (f32[32,24,128]{2,1,0:T(8,128)}, f32[32,24,128]{2,1,0:T(8,128)S(1)}, u32[]{:S(2)}, u32[]{:S(2)}) collective-permute-start(f32[32,24,128]{2,1,0:T(8,128)} %get-tuple-element.8), channel_id=1, source_target_pairs={{0,1},{1,0},{2,3},{3,2},{4,5},{5,4},{6,7},{7,6},{8,9},{9,8},{10,11... | collective-permute-start | bytes 1179656 | tf_op jit(solution)/shard_map/ppermute | solution.py:355

commit v3 on v2

--- a/solution.py
+++ b/solution.py
@@ -109,12 +109,17 @@
 
     row_bits = ROWS.bit_length() - 1
     batch_bits = batch.bit_length() - 1
-    wide = (groups * ROWS, virs)
+    quad = 4 * group_width
+    wide = (quad, virs)
     row = lax.broadcasted_iota(jnp.int32, wide, 0)
     col = lax.broadcasted_iota(jnp.int32, wide, 1)
-    inner = row & (ROWS - 1)
-    target = jnp.where(inner < group_width, (row >> row_bits) * group_width + inner, -1)
-    spread = jnp.where(col == target, 1.0, 0.0).astype(jnp.bfloat16)
+    low = (row >> 3) * group_width + (row & 7)
+    high = ((row - 32) >> 2) * group_width + 8 + (row & 3)
+    target = jnp.where(row < 32, low, high) - col
+    spread = jnp.concatenate(
+        [jnp.where(target == -start, 1.0, 0.0).astype(jnp.bfloat16) for start in range(0, virs, quad)],
+        axis=0,
+    )
 
     shape = (WINDOW * span, depth)
     row = lax.broadcasted_iota(jnp.int32, shape, 0) & (ROWS - 1)
@@ -175,10 +180,17 @@
             for q in range(p * part, (p + 1) * part, TILE):
                 fitted = jnp.dot(
                     right_t[...], half_buf[i, :, q : q + TILE], preferred_element_type=jnp.float32
-                ).astype(jnp.bfloat16)
-                fit_buf[:, i * ROWS : (i + 1) * ROWS, q : q + TILE] = fitted.reshape(
-                    groups, ROWS, TILE
                 )
+                for g in range(groups):
+                    start = g // 4 * quad
+                    low = fitted[start + g % 4 * 8 : start + g % 4 * 8 + 8, :]
+                    start += 32 + g % 4 // 2 * 8
+                    high = fitted[start : start + 8, :]
+                    if g % 2 == 1:
+                        high = pltpu.roll(high, 4, 0)
+                    fit_buf[g, i * ROWS : (i + 1) * ROWS, q : q + TILE] = jnp.concatenate(
+                        [low, high], axis=0
+                    ).astype(jnp.bfloat16)
 
     upper = batch // 2 * ROWS
     shape = (upper, LANES)
@@ -205,6 +217,10 @@
                 halves.append(jnp.concatenate([first[:8, :], mixed, second[:8, :]], axis=0))
             keep_ref[first_group + g] = jnp.where(own == 0, halves[0], halves[1])
             send_ref[first_group + g] = jnp.where(own == 0, halves[1], halves[0])
+
+
+def in_place(operand):
+    return pltpu.with_memory_space_constraint(operand, pltpu.HBM)
 
 
 def partial_sums(ints, blk_atoms, blk_count, occ_coeff, vir_coeff, batch_ids, groups):
@@ -233,7 +249,7 @@
             pltpu.VMEM((window_atoms * batch, depth), jnp.float32),
             pltpu.VMEM((window_atoms, batch * ROWS, depth), jnp.bfloat16),
             pltpu.VMEM((slots * ROWS, virs), jnp.bfloat16),
-            pltpu.VMEM((groups * ROWS, slots * ROWS), jnp.bfloat16),
+            pltpu.VMEM((virs, slots * ROWS), jnp.bfloat16),
             pltpu.VMEM((batch, slots * ROWS, aux_local), jnp.bfloat16),
             pltpu.VMEM((groups, batch * ROWS, aux_local), jnp.bfloat16),
             pltpu.SemaphoreType.DMA((3,)),
@@ -241,14 +257,14 @@
             pltpu.SemaphoreType.DMA((batch, WINDOW)),
             pltpu.SemaphoreType.DMA((WINDOW,)),
         ],
-        compiler_params=pltpu.CompilerParams(vmem_limit_bytes=63 * 1024 * 1024),
+        compiler_params=pltpu.CompilerParams(vmem_limit_bytes=40 * 1024 * 1024),
     )(
-        blk_atoms.T,
+        in_place(blk_atoms.T),
         blk_count,
-        batch_ids,
-        ints.reshape(slots, depth, aux_local),
-        occ_coeff,
-        vir_coeff,
+        in_place(batch_ids),
+        in_place(ints.reshape(slots, depth, aux_local)),
+        in_place(occ_coeff),
+        in_place(vir_coeff),
     )
 
 
@@ -293,7 +309,7 @@
         out_shape=jax.ShapeDtypeStruct((batch * group_width * batch, group_width), jnp.float32),
         in_specs=[pl.BlockSpec(memory_space=pltpu.VMEM)],
         out_specs=pl.BlockSpec(memory_space=pltpu.VMEM),
-    )(parts)
+    )(pltpu.with_memory_space_constraint(parts, pltpu.VMEM))
 
 
 def half_transform(left_rows, right_rows, block_ints, live_count):

time: 30.7 us -> 27 us (0.88)
  Pallas kernels: 10.6 us -> 8.2 us
  other arithmetic: 1.04 us -> 0.04 us
    pallas_call x1, Pallas kernels: 8.51 us -> 7.09 us  [partial_sums(): pl.pallas_call(functools.partial(partial_kernel, group_width), out_shape=...]
    convert_element_type x1, other arithmetic: 1.04 us -> 0.04 us  [on_device(): parts = (keep + lax.ppermute(send, 'aux', partners)).astype(jnp.bfloat16)]
    pallas_call x1, Pallas kernels: 2.04 us -> 1.11 us  [total_sums(): pl.pallas_call(functools.partial(total_kernel, group_width, batch), out_s...]
where the time goes in v3:
time: 27 us; the launch traced here: 26.7 us
  blocking collectives  15.9 us (59%)
  Pallas kernels  8.2 us (30%)
  waiting for transfers between devices  1.35 us (5%)
  between operations  0.66 us (2%)
  starting transfers between devices  0.51 us (2%)
    all_to_all x1, blocking collectives, on_device(): lax.all_to_all(parts, 'aux', split_axis=0, concat_axis=0, tiled=True)  15.9 us
    pallas_call x1, Pallas kernels, partial_sums(): pl.pallas_call(functools.partial(partial_kernel, group_width), out_shape=...  7.09 us
    ppermute x1, waiting for transfers between devices, on_device(): parts = (keep + lax.ppermute(send, 'aux', partners)).astype(jnp.bfloat16)  1.35 us
    pallas_call x1, Pallas kernels, total_sums(): pl.pallas_call(functools.partial(total_kernel, group_width, batch), out_s...  1.11 us
  transfers between devices with their start and end apart: 1, of which 1 were waited for; matrix products, arithmetic and copies ran while one was open for 0% of the time, Pallas kernels for 0%

profile of v3, /device:TPU:0, one launch (start us, length us, event | category | flops | bytes accessed | tf_op | source)
XLA Modules:
  0.0 26.7 jit_solution(12467506775479927755)
XLA Ops:
  0.7 7.1 %shard_map.64 = (f32[32,24,128]{2,1,0:T(8,128)S(1)}, f32[32,24,128]{2,1,0:T(8,128)S(1)}) custom-call(s32[2,32]{1,0:T(2,128)} %bitcast.6, s32[1]{0:T(128)S(6)} %copy.8.count_hbm, s32[8]{0:T(128)} %ids_hbm.1, bf16[32,256,512]{2,1,0:T(8,128)(2,1)} %bitcast.5, bf16[1280,4096]{1,0:T(8,128)(2,1)} %occ_hbm.1, bf16[4096,384]{1,0:T(8,128)(2,1)} %vir_hbm.1), custom_call_target="tpu_custom_call" | custom-call | tf_op jit(solution)/shard_map/pallas_call | solution.py:237
  7.8 0.5 %collective-permute-start = (f32[32,24,128]{2,1,0:T(8,128)S(1)}, f32[32,24,128]{2,1,0:T(8,128)S(1)}, u32[]{:S(2)}, u32[]{:S(2)}) collective-permute-start(f32[32,24,128]{2,1,0:T(8,128)S(1)} %get-tuple-element.8), channel_id=1, source_target_pairs={{0,1},{1,0},{2,3},{3,2},{4,5},{5,4},{6,7},{7,6},{8,9},{9,8},{10,11... | collective-permute-start | bytes 1179656 | tf_op jit(solution)/shard_map/ppermute | solution.py:371
  8.3 1.3 %collective-permute-done = f32[32,24,128]{2,1,0:T(8,128)S(1)} collective-permute-done((f32[32,24,128]{2,1,0:T(8,128)S(1)}, f32[32,24,128]{2,1,0:T(8,128)S(1)}, u32[]{:S(2)}, u32[]{:S(2)}) %collective-permute-start) | collective-permute-done | bytes 393248 | tf_op jit(solution)/shard_map/ppermute | solution.py:371
  9.7 15.9 %all_to_all.5.parts_ref = bf16[32,24,128]{2,1,0:T(8,128)(2,1)S(1)} all-to-all(bf16[32,24,128]{2,1,0:T(8,128)(2,1)S(1)} %add_convert_fusion), channel_id=1, replica_groups=mesh['aux'=32,'occ'=1] {'aux'}, dimensions={0} | all-to-all | bytes 393216 | tf_op jit(solution)/shard_map/all_to_all | solution.py:372
  25.6 1.1 %shard_map.65 = f32[768,12]{1,0:T(8,128)} custom-call(bf16[32,24,128]{2,1,0:T(8,128)(2,1)S(1)} %all_to_all.5.parts_ref), custom_call_target="tpu_custom_call" | custom-call | tf_op jit(solution)/shard_map/pallas_call | solution.py:307
  (1 shorter events, 0.0 us)
Async XLA Ops:
  7.8 1.9 %collective-permute-start = (f32[32,24,128]{2,1,0:T(8,128)S(1)}, f32[32,24,128]{2,1,0:T(8,128)S(1)}, u32[]{:S(2)}, u32[]{:S(2)}) collective-permute-start(f32[32,24,128]{2,1,0:T(8,128)S(1)} %get-tuple-element.8), channel_id=1, source_target_pairs={{0,1},{1,0},{2,3},{3,2},{4,5},{5,4},{6,7},{7,6},{8,9},{9,8},{10,11... | collective-permute-start | bytes 1179656 | tf_op jit(solution)/shard_map/ppermute | solution.py:371

commit v4 on v3

--- a/solution.py
+++ b/solution.py
@@ -17,8 +17,17 @@
 TILE = 256
 
 
+def device_order(count):
+    order = []
+    for plane in range(count // 8):
+        chips = (0, 1, 3, 2) if plane % 2 == 0 else (2, 3, 1, 0)
+        order += [plane * 8 + chip * 2 + core for chip in chips for core in range(2)]
+    return order if len(order) == count else list(range(count))
+
+
 def partial_kernel(
     group_width,
+    places,
     atoms_hbm,
     count_hbm,
     ids_hbm,
@@ -215,15 +224,16 @@
                 second = packed[(i + 1) * ROWS : (i + 2) * ROWS, :]
                 mixed = jnp.where(top_half, first[8:, :], pltpu.roll(second[8:, :], 4, 0))
                 halves.append(jnp.concatenate([first[:8, :], mixed, second[:8, :]], axis=0))
-            keep_ref[first_group + g] = jnp.where(own == 0, halves[0], halves[1])
-            send_ref[first_group + g] = jnp.where(own == 0, halves[1], halves[0])
+            keep_ref[places[first_group + g]] = jnp.where(own == 0, halves[0], halves[1])
+            send_ref[places[first_group + g]] = jnp.where(own == 0, halves[1], halves[0])
 
 
 def in_place(operand):
     return pltpu.with_memory_space_constraint(operand, pltpu.HBM)
 
 
-def partial_sums(ints, blk_atoms, blk_count, occ_coeff, vir_coeff, batch_ids, groups):
+def partial_sums(ints, blk_atoms, blk_count, occ_coeff, vir_coeff, batch_ids, places):
+    groups = len(places)
     slots, block, _, aux_local = ints.shape
     batch = batch_ids.shape[0]
     virs = vir_coeff.shape[1]
@@ -235,7 +245,7 @@
     far = pl.BlockSpec(memory_space=pltpu.HBM)
     result = jax.ShapeDtypeStruct((groups, batch // 4 * group_width, LANES), jnp.float32)
     return pl.pallas_call(
-        functools.partial(partial_kernel, group_width),
+        functools.partial(partial_kernel, group_width, places),
         out_shape=(result, result),
         in_specs=[far] * 6,
         out_specs=[pl.BlockSpec(memory_space=pltpu.VMEM)] * 2,
@@ -366,10 +376,14 @@
     batch = batch_ids.shape[0]
     groups = lax.axis_size("aux")
     group_width = vir_coeff.shape[1] // groups
-    keep, send = partial_sums(ints, blk_atoms, blk_count, occ_coeff, vir_coeff, batch_ids, groups)
+    order = device_order(groups)
+    places = [order.index(group) for group in range(groups)]
+    keep, send = partial_sums(ints, blk_atoms, blk_count, occ_coeff, vir_coeff, batch_ids, places)
     partners = [(owner, owner ^ 1) for owner in range(groups)]
     parts = (keep + lax.ppermute(send, "aux", partners)).astype(jnp.bfloat16)
-    parts = lax.all_to_all(parts, "aux", split_axis=0, concat_axis=0, tiled=True)
+    parts = lax.all_to_all(
+        parts, "aux", split_axis=0, concat_axis=0, tiled=True, axis_index_groups=[order]
+    )
     total = total_sums(parts, batch, group_width)
     return total.reshape(batch, 1, group_width, batch, group_width)
 

time: 27 us -> 26.7 us (0.989)
  no operation moved by 1% of the time
where the time goes in v4:
time: 26.7 us; the launch traced here: 26.5 us
  blocking collectives  15.7 us (59%)
  Pallas kernels  8.2 us (31%)
  waiting for transfers between devices  1.35 us (5%)
  between operations  0.66 us (2%)
  starting transfers between devices  0.51 us (2%)
    all_to_all x1, blocking collectives, on_device(): lax.all_to_all(parts, 'aux', split_axis=0, concat_axis=0, tiled=True, axi...  15.7 us
    pallas_call x1, Pallas kernels, partial_sums(): pl.pallas_call(functools.partial(partial_kernel, group_width, places), ou...  7.09 us
    ppermute x1, waiting for transfers between devices, on_device(): parts = (keep + lax.ppermute(send, 'aux', partners)).astype(jnp.bfloat16)  1.35 us
    pallas_call x1, Pallas kernels, total_sums(): pl.pallas_call(functools.partial(total_kernel, group_width, batch), out_s...  1.11 us
  transfers between devices with their start and end apart: 1, of which 1 were waited for; matrix products, arithmetic and copies ran while one was open for 0% of the time, Pallas kernels for 0%

profile of v4, /device:TPU:0, one launch (start us, length us, event | category | flops | bytes accessed | tf_op | source)
XLA Modules:
  0.0 26.5 jit_solution(14568456209399161439)
XLA Ops:
  0.7 7.1 %shard_map.64 = (f32[32,24,128]{2,1,0:T(8,128)S(1)}, f32[32,24,128]{2,1,0:T(8,128)S(1)}) custom-call(s32[2,32]{1,0:T(2,128)} %bitcast.6, s32[1]{0:T(128)S(6)} %copy.8.count_hbm, s32[8]{0:T(128)} %ids_hbm.1, bf16[32,256,512]{2,1,0:T(8,128)(2,1)} %bitcast.5, bf16[1280,4096]{1,0:T(8,128)(2,1)} %occ_hbm.1, bf16[4096,384]{1,0:T(8,128)(2,1)} %vir_hbm.1), custom_call_target="tpu_custom_call" | custom-call | tf_op jit(solution)/shard_map/pallas_call | solution.py:247
  7.8 0.5 %collective-permute-start = (f32[32,24,128]{2,1,0:T(8,128)S(1)}, f32[32,24,128]{2,1,0:T(8,128)S(1)}, u32[]{:S(2)}, u32[]{:S(2)}) collective-permute-start(f32[32,24,128]{2,1,0:T(8,128)S(1)} %get-tuple-element.8), channel_id=1, source_target_pairs={{0,1},{1,0},{2,3},{3,2},{4,5},{5,4},{6,7},{7,6},{8,9},{9,8},{10,11... | collective-permute-start | bytes 1179656 | tf_op jit(solution)/shard_map/ppermute | solution.py:383
  8.3 1.3 %collective-permute-done = f32[32,24,128]{2,1,0:T(8,128)S(1)} collective-permute-done((f32[32,24,128]{2,1,0:T(8,128)S(1)}, f32[32,24,128]{2,1,0:T(8,128)S(1)}, u32[]{:S(2)}, u32[]{:S(2)}) %collective-permute-start) | collective-permute-done | bytes 393248 | tf_op jit(solution)/shard_map/ppermute | solution.py:383
  9.7 15.7 %all_to_all.5.parts_ref = bf16[32,24,128]{2,1,0:T(8,128)(2,1)S(1)} all-to-all(bf16[32,24,128]{2,1,0:T(8,128)(2,1)S(1)} %add_convert_fusion), channel_id=1, replica_groups={{0,1,2,3,6,7,4,5,12,13,14,15,10,11,8,9,16,17,18,19,22,23,20,21,28,29,30..., dimensions={0} | all-to-all | bytes 393216 | tf_op jit(solution)/shard_map/all_to_all | solution.py:384
  25.4 1.1 %shard_map.65 = f32[768,12]{1,0:T(8,128)} custom-call(bf16[32,24,128]{2,1,0:T(8,128)(2,1)S(1)} %all_to_all.5.parts_ref), custom_call_target="tpu_custom_call" | custom-call | tf_op jit(solution)/shard_map/pallas_call | solution.py:317
  (1 shorter events, 0.0 us)
Async XLA Ops:
  7.8 1.9 %collective-permute-start = (f32[32,24,128]{2,1,0:T(8,128)S(1)}, f32[32,24,128]{2,1,0:T(8,128)S(1)}, u32[]{:S(2)}, u32[]{:S(2)}) collective-permute-start(f32[32,24,128]{2,1,0:T(8,128)S(1)} %get-tuple-element.8), channel_id=1, source_target_pairs={{0,1},{1,0},{2,3},{3,2},{4,5},{5,4},{6,7},{7,6},{8,9},{9,8},{10,11... | collective-permute-start | bytes 1179656 | tf_op jit(solution)/shard_map/ppermute | solution.py:383

commit v5 on v4

--- a/solution.py
+++ b/solution.py
@@ -225,7 +225,9 @@
                 mixed = jnp.where(top_half, first[8:, :], pltpu.roll(second[8:, :], 4, 0))
                 halves.append(jnp.concatenate([first[:8, :], mixed, second[:8, :]], axis=0))
             keep_ref[places[first_group + g]] = jnp.where(own == 0, halves[0], halves[1])
-            send_ref[places[first_group + g]] = jnp.where(own == 0, halves[1], halves[0])
+            send_ref[places[first_group + g]] = jnp.where(own == 0, halves[1], halves[0]).astype(
+                jnp.bfloat16
+            )
 
 
 def in_place(operand):
@@ -243,10 +245,13 @@
     depth = block * block
     group_width = virs // groups
     far = pl.BlockSpec(memory_space=pltpu.HBM)
-    result = jax.ShapeDtypeStruct((groups, batch // 4 * group_width, LANES), jnp.float32)
+    shape = (groups, batch // 4 * group_width, LANES)
     return pl.pallas_call(
         functools.partial(partial_kernel, group_width, places),
-        out_shape=(result, result),
+        out_shape=(
+            jax.ShapeDtypeStruct(shape, jnp.float32),
+            jax.ShapeDtypeStruct(shape, jnp.bfloat16),
+        ),
         in_specs=[far] * 6,
         out_specs=[pl.BlockSpec(memory_space=pltpu.VMEM)] * 2,
         scratch_shapes=[

time: 26.7 us -> 26.4 us (0.989)
  waiting for transfers between devices: 1.35 us -> 1.07 us
    ppermute x1, waiting for transfers between devices: 1.35 us -> 1.07 us  [on_device(): parts = (keep + lax.ppermute(send, 'aux', partners)).astype(jnp.bfloat16)]
where the time goes in v5:
time: 26.4 us; the launch traced here: 26.2 us
  blocking collectives  15.7 us (59%)
  Pallas kernels  8.21 us (31%)
  waiting for transfers between devices  1.07 us (4%)
  between operations  0.66 us (2%)
  starting transfers between devices  0.51 us (2%)
    all_to_all x1, blocking collectives, on_device(): lax.all_to_all(parts, 'aux', split_axis=0, concat_axis=0, tiled=True, axi...  15.7 us
    pallas_call x1, Pallas kernels, partial_sums(): pl.pallas_call(functools.partial(partial_kernel, group_width, places), ou...  7.09 us
    pallas_call x1, Pallas kernels, total_sums(): pl.pallas_call(functools.partial(total_kernel, group_width, batch), out_s...  1.11 us
    ppermute x1, waiting for transfers between devices, on_device(): parts = (keep + lax.ppermute(send, 'aux', partners)).astype(jnp.bfloat16)  1.07 us
  transfers between devices with their start and end apart: 1, of which 1 were waited for; matrix products, arithmetic and copies ran while one was open for 0% of the time, Pallas kernels for 0%

profile of v5, /device:TPU:0, one launch (start us, length us, event | category | flops | bytes accessed | tf_op | source)
XLA Modules:
  0.0 26.2 jit_solution(8888955538162319935)
XLA Ops:
  0.7 7.1 %shard_map.64 = (f32[32,24,128]{2,1,0:T(8,128)S(1)}, bf16[32,24,128]{2,1,0:T(8,128)(2,1)S(1)}) custom-call(s32[2,32]{1,0:T(2,128)} %bitcast.6, s32[1]{0:T(128)S(6)} %copy.8.count_hbm, s32[8]{0:T(128)} %ids_hbm.1, bf16[32,256,512]{2,1,0:T(8,128)(2,1)} %bitcast.5, bf16[1280,4096]{1,0:T(8,128)(2,1)} %occ_hbm.1, bf16[4096,384]{1,0:T(8,128)(2,1)} %vir_hbm.1), custom_call_target="tpu_custom_call" | custom-call | tf_op jit(solution)/shard_map/pallas_call | solution.py:249
  7.8 0.5 %collective-permute-start = (bf16[32,24,128]{2,1,0:T(8,128)(2,1)S(1)}, bf16[32,24,128]{2,1,0:T(8,128)(2,1)S(1)}, u32[]{:S(2)}, u32[]{:S(2)}) collective-permute-start(bf16[32,24,128]{2,1,0:T(8,128)(2,1)S(1)} %get-tuple-element.8), channel_id=1, source_target_pairs={{0,1},{1,0},{2,3},{3,2},{4,5},{5,4},{6,7},{7,6},{8,9},{9,8},{10,11... | collective-permute-start | bytes 589832 | tf_op jit(solution)/shard_map/ppermute | solution.py:388
  8.3 1.1 %collective-permute-done = bf16[32,24,128]{2,1,0:T(8,128)(2,1)S(1)} collective-permute-done((bf16[32,24,128]{2,1,0:T(8,128)(2,1)S(1)}, bf16[32,24,128]{2,1,0:T(8,128)(2,1)S(1)}, u32[]{:S(2)}, u32[]{:S(2)}) %collective-permute-start) | collective-permute-done | bytes 196640 | tf_op jit(solution)/shard_map/ppermute | solution.py:388
  9.3 0.1 add_convert_fusion
  9.4 15.7 %all_to_all.5.parts_ref = bf16[32,24,128]{2,1,0:T(8,128)(2,1)S(1)} all-to-all(bf16[32,24,128]{2,1,0:T(8,128)(2,1)S(1)} %add_convert_fusion), channel_id=1, replica_groups={{0,1,2,3,6,7,4,5,12,13,14,15,10,11,8,9,16,17,18,19,22,23,20,21,28,29,30..., dimensions={0} | all-to-all | bytes 393216 | tf_op jit(solution)/shard_map/all_to_all | solution.py:389
  25.1 1.1 %shard_map.65 = f32[768,12]{1,0:T(8,128)} custom-call(bf16[32,24,128]{2,1,0:T(8,128)(2,1)S(1)} %all_to_all.5.parts_ref), custom_call_target="tpu_custom_call" | custom-call | tf_op jit(solution)/shard_map/pallas_call | solution.py:322
Async XLA Ops:
  7.8 1.6 %collective-permute-start = (bf16[32,24,128]{2,1,0:T(8,128)(2,1)S(1)}, bf16[32,24,128]{2,1,0:T(8,128)(2,1)S(1)}, u32[]{:S(2)}, u32[]{:S(2)}) collective-permute-start(bf16[32,24,128]{2,1,0:T(8,128)(2,1)S(1)} %get-tuple-element.8), channel_id=1, source_target_pairs={{0,1},{1,0},{2,3},{3,2},{4,5},{5,4},{6,7},{7,6},{8,9},{9,8},{10,11... | collective-permute-start | bytes 589832 | tf_op jit(solution)/shard_map/ppermute | solution.py:388

commit v6 on v5

--- a/solution.py
+++ b/solution.py
@@ -29,7 +29,7 @@
     group_width,
     places,
     atoms_hbm,
-    count_hbm,
+    count_ref,
     ids_hbm,
     ints_hbm,
     occ_hbm,
@@ -37,7 +37,6 @@
     keep_ref,
     send_ref,
     atoms_ref,
-    count_ref,
     ids_ref,
     ints_buf,
     occ_buf,
@@ -69,7 +68,7 @@
     small_copies = [
         pltpu.make_async_copy(source, target, small_sem.at[s])
         for s, (source, target) in enumerate(
-            ((ids_hbm, ids_ref), (atoms_hbm, atoms_ref), (count_hbm, count_ref))
+            ((ids_hbm, ids_ref), (atoms_hbm, atoms_ref))
         )
     ]
     for copy in small_copies:
@@ -208,26 +207,26 @@
     from_below = (col < upper) & (col > row)
     top_half = lax.broadcasted_iota(jnp.int32, (8, LANES), 0) < 4
     own = lax.rem(me, 2)
-    high = batch * ROWS
+    size = batch * ROWS
     for first_group in range(0, groups, 2):
-        both = fit_buf[first_group : first_group + 2].reshape(2 * high, aux_local)
+        both = fit_buf[first_group : first_group + 2].reshape(2 * size, aux_local)
         grams = lax.dot_general(
             both, both, (((1,), (1,)), ((), ())), preferred_element_type=jnp.float32
         )
+        halves = [], []
         for g in range(2):
-            gram = grams[g * high : (g + 1) * high, g * high : (g + 1) * high]
+            gram = grams[g * size : (g + 1) * size, g * size : (g + 1) * size]
             below = pltpu.roll(gram[upper:, :], upper + 1, 1)
             packed = jnp.where(from_below, below, gram[:upper, :])
-            halves = []
             for i in range(0, batch // 2, 2):
                 first = packed[i * ROWS : (i + 1) * ROWS, :]
                 second = packed[(i + 1) * ROWS : (i + 2) * ROWS, :]
                 mixed = jnp.where(top_half, first[8:, :], pltpu.roll(second[8:, :], 4, 0))
-                halves.append(jnp.concatenate([first[:8, :], mixed, second[:8, :]], axis=0))
-            keep_ref[places[first_group + g]] = jnp.where(own == 0, halves[0], halves[1])
-            send_ref[places[first_group + g]] = jnp.where(own == 0, halves[1], halves[0]).astype(
-                jnp.bfloat16
-            )
+                halves[i // 2].extend([first[:8, :], mixed, second[:8, :]])
+        low, high = (jnp.concatenate(half, axis=0) for half in halves)
+        place = places[first_group] // 2
+        keep_ref[place] = jnp.where(own == 0, low, high)
+        send_ref[place] = jnp.where(own == 0, high, low).astype(jnp.bfloat16)
 
 
 def in_place(operand):
@@ -245,18 +244,17 @@
     depth = block * block
     group_width = virs // groups
     far = pl.BlockSpec(memory_space=pltpu.HBM)
-    shape = (groups, batch // 4 * group_width, LANES)
+    shape = (groups // 2, batch // 2 * group_width, LANES)
     return pl.pallas_call(
         functools.partial(partial_kernel, group_width, places),
         out_shape=(
             jax.ShapeDtypeStruct(shape, jnp.float32),
             jax.ShapeDtypeStruct(shape, jnp.bfloat16),
         ),
-        in_specs=[far] * 6,
+        in_specs=[far, pl.BlockSpec(memory_space=pltpu.SMEM)] + [far] * 4,
         out_specs=[pl.BlockSpec(memory_space=pltpu.VMEM)] * 2,
         scratch_shapes=[
             pltpu.SMEM((2, slots), jnp.int32),
-            pltpu.SMEM((1,), jnp.int32),
             pltpu.SMEM((batch,), jnp.int32),
             pltpu.VMEM((slots, depth, aux_local), jnp.bfloat16),
             pltpu.VMEM((batch, ROWS, WINDOW * span), jnp.bfloat16),
@@ -267,7 +265,7 @@
             pltpu.VMEM((virs, slots * ROWS), jnp.bfloat16),
             pltpu.VMEM((batch, slots * ROWS, aux_local), jnp.bfloat16),
             pltpu.VMEM((groups, batch * ROWS, aux_local), jnp.bfloat16),
-            pltpu.SemaphoreType.DMA((3,)),
+            pltpu.SemaphoreType.DMA((2,)),
             pltpu.SemaphoreType.DMA((PARTS, CHUNKS)),
             pltpu.SemaphoreType.DMA((batch, WINDOW)),
             pltpu.SemaphoreType.DMA((WINDOW,)),
@@ -283,11 +281,8 @@
     )
 
 
-def total_kernel(group_width, batch, parts_ref, out_ref):
-    owners, rows, _ = parts_ref.shape
-    total = jnp.sum(
-        parts_ref[...].astype(jnp.float32).reshape(owners // 2, 2 * rows, LANES), axis=0
-    )
+def total_kernel(group_width, batch, parts_ref, out_hbm, out_buf, out_sem):
+    total = jnp.sum(parts_ref[...].astype(jnp.float32), axis=0)
     upper = batch // 2 * ROWS
     top_half = lax.broadcasted_iota(jnp.int32, (8, LANES), 0) < 4
     pieces = []
@@ -308,6 +303,7 @@
     col = lax.broadcasted_iota(jnp.int32, shape, 1)
     direct = ((row < upper) & ((col >= upper) | (col <= row))) | ((row >= upper) & (col >= row))
     whole = jnp.where(direct, both, both.T)
+    copies = []
     for i in range(batch):
         for c in range(0, group_width, 8):
             rows = whole[i * ROWS + c : i * ROWS + c + 8, :]
@@ -315,15 +311,31 @@
             for j in range(batch):
                 moved = rows if j == 0 else pltpu.roll(rows, LANES - j * ROWS, 1)
                 start = (i * group_width + c) * batch + j
-                out_ref[pl.ds(start, count, stride=batch), :] = moved[:count, :group_width]
+                out_buf[pl.ds(start, count, stride=batch), :] = moved[:count, :group_width]
+        if (i + 1) % (batch // 2) == 0:
+            size = batch // 2 * group_width * batch
+            block = pl.ds(len(copies) * size, size)
+            copies.append(
+                pltpu.make_async_copy(
+                    out_buf.at[block, :], out_hbm.at[block, :], out_sem.at[len(copies)]
+                )
+            )
+            copies[-1].start()
+    for copy in copies:
+        copy.wait()
 
 
 def total_sums(parts, batch, group_width):
+    rows = batch * group_width * batch
     return pl.pallas_call(
         functools.partial(total_kernel, group_width, batch),
-        out_shape=jax.ShapeDtypeStruct((batch * group_width * batch, group_width), jnp.float32),
+        out_shape=jax.ShapeDtypeStruct((rows, group_width), jnp.float32),
         in_specs=[pl.BlockSpec(memory_space=pltpu.VMEM)],
-        out_specs=pl.BlockSpec(memory_space=pltpu.VMEM),
+        out_specs=pl.BlockSpec(memory_space=pltpu.HBM),
+        scratch_shapes=[
+            pltpu.VMEM((rows + 8 * batch, group_width), jnp.float32),
+            pltpu.SemaphoreType.DMA((2,)),
+        ],
     )(pltpu.with_memory_space_constraint(parts, pltpu.VMEM))
 
 
@@ -386,9 +398,15 @@
     keep, send = partial_sums(ints, blk_atoms, blk_count, occ_coeff, vir_coeff, batch_ids, places)
     partners = [(owner, owner ^ 1) for owner in range(groups)]
     parts = (keep + lax.ppermute(send, "aux", partners)).astype(jnp.bfloat16)
+    pair_shape = parts.shape
     parts = lax.all_to_all(
-        parts, "aux", split_axis=0, concat_axis=0, tiled=True, axis_index_groups=[order]
-    )
+        parts.reshape(groups, -1, LANES),
+        "aux",
+        split_axis=0,
+        concat_axis=0,
+        tiled=True,
+        axis_index_groups=[order],
+    ).reshape(pair_shape)
     total = total_sums(parts, batch, group_width)
     return total.reshape(batch, 1, group_width, batch, group_width)
 

time: 26.4 us -> 26.4 us (level)
  no operation moved by 1% of the time
where the time goes in v6:
time: 26.4 us; the launch traced here: 26.2 us
  blocking collectives  15.7 us (59%)
  Pallas kernels  8.15 us (31%)
  waiting for transfers between devices  1.07 us (4%)
  between operations  0.66 us (2%)
  starting transfers between devices  0.52 us (2%)
    all_to_all x1, blocking collectives, on_device(): lax.all_to_all(parts.reshape(groups, -1, LANES), 'aux', split_axis=0, con...  15.7 us
    pallas_call x1, Pallas kernels, partial_sums(): pl.pallas_call(functools.partial(partial_kernel, group_width, places), ou...  7.08 us
    ppermute x1, waiting for transfers between devices, on_device(): parts = (keep + lax.ppermute(send, 'aux', partners)).astype(jnp.bfloat16)  1.07 us
    pallas_call x1, Pallas kernels, total_sums(): pl.pallas_call(functools.partial(total_kernel, group_width, batch), out_s...  1.07 us
  transfers between devices with their start and end apart: 1, of which 1 were waited for; matrix products, arithmetic and copies ran while one was open for 0% of the time, Pallas kernels for 0%

profile of v6, /device:TPU:0, one launch (start us, length us, event | category | flops | bytes accessed | tf_op | source)
XLA Modules:
  0.0 26.2 jit_solution(15661389408030192952)
XLA Ops:
  0.7 7.1 %shard_map.64 = (f32[16,48,128]{2,1,0:T(8,128)S(1)}, bf16[16,48,128]{2,1,0:T(8,128)(2,1)S(1)}) custom-call(s32[2,32]{1,0:T(2,128)} %bitcast.10, s32[1]{0:T(128)S(6)} %copy.8.count_ref, s32[8]{0:T(128)} %ids_hbm.1, bf16[32,256,512]{2,1,0:T(8,128)(2,1)} %bitcast.8, bf16[1280,4096]{1,0:T(8,128)(2,1)} %occ_hbm.1, bf16[4096,384]{1,0:T(8,128)(2,1)} %vir_hbm.1), custom_call_target="tpu_custom_call" | custom-call | tf_op jit(solution)/shard_map/pallas_call | solution.py:248
  7.7 0.5 %collective-permute-start = (bf16[16,48,128]{2,1,0:T(8,128)(2,1)S(1)}, bf16[16,48,128]{2,1,0:T(8,128)(2,1)S(1)}, u32[]{:S(2)}, u32[]{:S(2)}) collective-permute-start(bf16[16,48,128]{2,1,0:T(8,128)(2,1)S(1)} %get-tuple-element.8), channel_id=1, source_target_pairs={{0,1},{1,0},{2,3},{3,2},{4,5},{5,4},{6,7},{7,6},{8,9},{9,8},{10,11... | collective-permute-start | bytes 589832 | tf_op jit(solution)/shard_map/ppermute | solution.py:400
  8.3 1.1 %collective-permute-done = bf16[16,48,128]{2,1,0:T(8,128)(2,1)S(1)} collective-permute-done((bf16[16,48,128]{2,1,0:T(8,128)(2,1)S(1)}, bf16[16,48,128]{2,1,0:T(8,128)(2,1)S(1)}, u32[]{:S(2)}, u32[]{:S(2)}) %collective-permute-start) | collective-permute-done | bytes 196640 | tf_op jit(solution)/shard_map/ppermute | solution.py:400
  9.3 0.1 add_convert_fusion
  9.4 15.7 %all_to_all.5 = bf16[32,24,128]{2,1,0:T(8,128)(2,1)S(1)} all-to-all(bf16[32,24,128]{2,1,0:T(8,128)(2,1)S(1)} %bitcast.9), channel_id=1, replica_groups={{0,1,2,3,6,7,4,5,12,13,14,15,10,11,8,9,16,17,18,19,22,23,20,21,28,29,30..., dimensions={0} | all-to-all | bytes 393216 | tf_op jit(solution)/shard_map/all_to_all | solution.py:402
  25.1 1.1 %shard_map.65 = f32[768,12]{1,0:T(8,128)} custom-call(bf16[16,48,128]{2,1,0:T(8,128)(2,1)S(1)} %bitcast.7), custom_call_target="tpu_custom_call" | custom-call | tf_op jit(solution)/shard_map/pallas_call | solution.py:330
Async XLA Ops:
  7.7 1.6 %collective-permute-start = (bf16[16,48,128]{2,1,0:T(8,128)(2,1)S(1)}, bf16[16,48,128]{2,1,0:T(8,128)(2,1)S(1)}, u32[]{:S(2)}, u32[]{:S(2)}) collective-permute-start(bf16[16,48,128]{2,1,0:T(8,128)(2,1)S(1)} %get-tuple-element.8), channel_id=1, source_target_pairs={{0,1},{1,0},{2,3},{3,2},{4,5},{5,4},{6,7},{7,6},{8,9},{9,8},{10,11... | collective-permute-start | bytes 589832 | tf_op jit(solution)/shard_map/ppermute | solution.py:400

commit v7 on v6

--- a/solution.py
+++ b/solution.py
@@ -10,7 +10,7 @@
 LANES = 128
 ROWS = 16
 WINDOW = 3
-CHUNKS = 1
+CHUNKS = ((16, 16), (32,))
 PARTS = 2
 EARLY = 1
 PRIO = 1
@@ -62,7 +62,6 @@
     span = occ_hbm.shape[1] // owners
     span_atoms = span // ROWS
     window_atoms = left_big.shape[0]
-    step = slots // CHUNKS
     part = aux_local // PARTS
 
     small_copies = [
@@ -80,17 +79,23 @@
         )
         for b in range(WINDOW)
     ]
+    ints_copies = []
+    pieces = []
+    for p, sizes in enumerate(CHUNKS):
+        start = 0
+        for size in sizes:
+            block = (pl.ds(start, size), slice(None), pl.ds(p * part, part))
+            ints_copies.append(
+                pltpu.make_async_copy(
+                    ints_hbm.at[block], ints_buf.at[block], ints_sem.at[len(ints_copies)]
+                )
+            )
+            pieces.append((p, start, start + size))
+            start += size
+    for copy in ints_copies[:EARLY]:
+        copy.start(priority=PRIO)
     for copy in vir_copies:
         copy.start()
-    ints_copies = []
-    for p in range(PARTS):
-        for c in range(CHUNKS):
-            block = (pl.ds(c * step, step), slice(None), pl.ds(p * part, part))
-            ints_copies.append(
-                pltpu.make_async_copy(ints_hbm.at[block], ints_buf.at[block], ints_sem.at[p, c])
-            )
-    for copy in ints_copies[:EARLY]:
-        copy.start(priority=PRIO)
     small_copies[0].wait()
     occ_copies = []
     for i in range(batch):
@@ -176,9 +181,11 @@
 
     for p in range(PARTS):
         cols = slice(p * part, (p + 1) * part)
-        for c in range(CHUNKS):
-            ints_copies[p * CHUNKS + c].wait()
-            for k in range(c * step, (c + 1) * step):
+        for copy, (piece_part, first, last) in zip(ints_copies, pieces):
+            if piece_part != p:
+                continue
+            copy.wait()
+            for k in range(first, last):
                 half = jnp.dot(
                     left_big[near(k, 0)], ints_buf[k, :, cols], preferred_element_type=jnp.float32
                 ).astype(jnp.bfloat16)
@@ -266,7 +273,7 @@
             pltpu.VMEM((batch, slots * ROWS, aux_local), jnp.bfloat16),
             pltpu.VMEM((groups, batch * ROWS, aux_local), jnp.bfloat16),
             pltpu.SemaphoreType.DMA((2,)),
-            pltpu.SemaphoreType.DMA((PARTS, CHUNKS)),
+            pltpu.SemaphoreType.DMA((sum(map(len, CHUNKS)),)),
             pltpu.SemaphoreType.DMA((batch, WINDOW)),
             pltpu.SemaphoreType.DMA((WINDOW,)),
         ],

time: 26.4 us -> 26.2 us (level)
  no operation moved by 1% of the time
where the time goes in v7:
time: 26.2 us; the launch traced here: 26 us
  blocking collectives  15.7 us (60%)
  Pallas kernels  7.97 us (30%)
  waiting for transfers between devices  1.07 us (4%)
  between operations  0.66 us (3%)
  starting transfers between devices  0.52 us (2%)
    all_to_all x1, blocking collectives, on_device(): lax.all_to_all(parts.reshape(groups, -1, LANES), 'aux', split_axis=0, con...  15.7 us
    pallas_call x1, Pallas kernels, partial_sums(): pl.pallas_call(functools.partial(partial_kernel, group_width, places), ou...  6.91 us
    ppermute x1, waiting for transfers between devices, on_device(): parts = (keep + lax.ppermute(send, 'aux', partners)).astype(jnp.bfloat16)  1.07 us
    pallas_call x1, Pallas kernels, total_sums(): pl.pallas_call(functools.partial(total_kernel, group_width, batch), out_s...  1.07 us
  transfers between devices with their start and end apart: 1, of which 1 were waited for; matrix products, arithmetic and copies ran while one was open for 0% of the time, Pallas kernels for 0%

profile of v7, /device:TPU:0, one launch (start us, length us, event | category | flops | bytes accessed | tf_op | source)
XLA Modules:
  0.0 26.0 jit_solution(416780917583854118)
XLA Ops:
  0.7 6.9 %shard_map.64 = (f32[16,48,128]{2,1,0:T(8,128)S(1)}, bf16[16,48,128]{2,1,0:T(8,128)(2,1)S(1)}) custom-call(s32[2,32]{1,0:T(2,128)} %bitcast.10, s32[1]{0:T(128)S(6)} %copy.8.count_ref, s32[8]{0:T(128)} %ids_hbm.1, bf16[32,256,512]{2,1,0:T(8,128)(2,1)} %bitcast.8, bf16[1280,4096]{1,0:T(8,128)(2,1)} %occ_hbm.1, bf16[4096,384]{1,0:T(8,128)(2,1)} %vir_hbm.1), custom_call_target="tpu_custom_call" | custom-call | tf_op jit(solution)/shard_map/pallas_call | solution.py:255
  7.6 0.5 %collective-permute-start = (bf16[16,48,128]{2,1,0:T(8,128)(2,1)S(1)}, bf16[16,48,128]{2,1,0:T(8,128)(2,1)S(1)}, u32[]{:S(2)}, u32[]{:S(2)}) collective-permute-start(bf16[16,48,128]{2,1,0:T(8,128)(2,1)S(1)} %get-tuple-element.8), channel_id=1, source_target_pairs={{0,1},{1,0},{2,3},{3,2},{4,5},{5,4},{6,7},{7,6},{8,9},{9,8},{10,11... | collective-permute-start | bytes 589832 | tf_op jit(solution)/shard_map/ppermute | solution.py:407
  8.1 1.1 %collective-permute-done = bf16[16,48,128]{2,1,0:T(8,128)(2,1)S(1)} collective-permute-done((bf16[16,48,128]{2,1,0:T(8,128)(2,1)S(1)}, bf16[16,48,128]{2,1,0:T(8,128)(2,1)S(1)}, u32[]{:S(2)}, u32[]{:S(2)}) %collective-permute-start) | collective-permute-done | bytes 196640 | tf_op jit(solution)/shard_map/ppermute | solution.py:407
  9.2 0.1 add_convert_fusion
  9.2 15.7 %all_to_all.5 = bf16[32,24,128]{2,1,0:T(8,128)(2,1)S(1)} all-to-all(bf16[32,24,128]{2,1,0:T(8,128)(2,1)S(1)} %bitcast.9), channel_id=1, replica_groups={{0,1,2,3,6,7,4,5,12,13,14,15,10,11,8,9,16,17,18,19,22,23,20,21,28,29,30..., dimensions={0} | all-to-all | bytes 393216 | tf_op jit(solution)/shard_map/all_to_all | solution.py:409
  24.9 1.1 %shard_map.65 = f32[768,12]{1,0:T(8,128)} custom-call(bf16[16,48,128]{2,1,0:T(8,128)(2,1)S(1)} %bitcast.7), custom_call_target="tpu_custom_call" | custom-call | tf_op jit(solution)/shard_map/pallas_call | solution.py:337
Async XLA Ops:
  7.6 1.6 %collective-permute-start = (bf16[16,48,128]{2,1,0:T(8,128)(2,1)S(1)}, bf16[16,48,128]{2,1,0:T(8,128)(2,1)S(1)}, u32[]{:S(2)}, u32[]{:S(2)}) collective-permute-start(bf16[16,48,128]{2,1,0:T(8,128)(2,1)S(1)} %get-tuple-element.8), channel_id=1, source_target_pairs={{0,1},{1,0},{2,3},{3,2},{4,5},{5,4},{6,7},{7,6},{8,9},{9,8},{10,11... | collective-permute-start | bytes 589832 | tf_op jit(solution)/shard_map/ppermute | solution.py:407

commit v8 on v7

--- a/solution.py
+++ b/solution.py
@@ -70,8 +70,6 @@
             ((ids_hbm, ids_ref), (atoms_hbm, atoms_ref))
         )
     ]
-    for copy in small_copies:
-        copy.start()
     starts = [pl.multiple_of(lax.rem(me + b, owners) * span, LANES) for b in range(WINDOW)]
     vir_copies = [
         pltpu.make_async_copy(
@@ -94,6 +92,8 @@
             start += size
     for copy in ints_copies[:EARLY]:
         copy.start(priority=PRIO)
+    for copy in small_copies:
+        copy.start()
     for copy in vir_copies:
         copy.start()
     small_copies[0].wait()

time: 26.2 us -> 26.2 us (level)
  no operation moved by 1% of the time
where the time goes in v8:
time: 26.2 us; the launch traced here: 26 us
  blocking collectives  15.7 us (60%)
  Pallas kernels  7.96 us (30%)
  waiting for transfers between devices  1.07 us (4%)
  between operations  0.66 us (3%)
  starting transfers between devices  0.52 us (2%)
    all_to_all x1, blocking collectives, on_device(): lax.all_to_all(parts.reshape(groups, -1, LANES), 'aux', split_axis=0, con...  15.7 us
    pallas_call x1, Pallas kernels, partial_sums(): pl.pallas_call(functools.partial(partial_kernel, group_width, places), ou...  6.9 us
    ppermute x1, waiting for transfers between devices, on_device(): parts = (keep + lax.ppermute(send, 'aux', partners)).astype(jnp.bfloat16)  1.07 us
    pallas_call x1, Pallas kernels, total_sums(): pl.pallas_call(functools.partial(total_kernel, group_width, batch), out_s...  1.07 us
  transfers between devices with their start and end apart: 1, of which 1 were waited for; matrix products, arithmetic and copies ran while one was open for 0% of the time, Pallas kernels for 0%

profile of v8, /device:TPU:0, one launch (start us, length us, event | category | flops | bytes accessed | tf_op | source)
XLA Modules:
  0.0 26.0 jit_solution(12542048163950334322)
XLA Ops:
  0.7 6.9 %shard_map.64 = (f32[16,48,128]{2,1,0:T(8,128)S(1)}, bf16[16,48,128]{2,1,0:T(8,128)(2,1)S(1)}) custom-call(s32[2,32]{1,0:T(2,128)} %bitcast.10, s32[1]{0:T(128)S(6)} %copy.8.count_ref, s32[8]{0:T(128)} %ids_hbm.1, bf16[32,256,512]{2,1,0:T(8,128)(2,1)} %bitcast.8, bf16[1280,4096]{1,0:T(8,128)(2,1)} %occ_hbm.1, bf16[4096,384]{1,0:T(8,128)(2,1)} %vir_hbm.1), custom_call_target="tpu_custom_call" | custom-call | tf_op jit(solution)/shard_map/pallas_call | solution.py:255
  7.6 0.5 %collective-permute-start = (bf16[16,48,128]{2,1,0:T(8,128)(2,1)S(1)}, bf16[16,48,128]{2,1,0:T(8,128)(2,1)S(1)}, u32[]{:S(2)}, u32[]{:S(2)}) collective-permute-start(bf16[16,48,128]{2,1,0:T(8,128)(2,1)S(1)} %get-tuple-element.8), channel_id=1, source_target_pairs={{0,1},{1,0},{2,3},{3,2},{4,5},{5,4},{6,7},{7,6},{8,9},{9,8},{10,11... | collective-permute-start | bytes 589832 | tf_op jit(solution)/shard_map/ppermute | solution.py:407
  8.1 1.1 %collective-permute-done = bf16[16,48,128]{2,1,0:T(8,128)(2,1)S(1)} collective-permute-done((bf16[16,48,128]{2,1,0:T(8,128)(2,1)S(1)}, bf16[16,48,128]{2,1,0:T(8,128)(2,1)S(1)}, u32[]{:S(2)}, u32[]{:S(2)}) %collective-permute-start) | collective-permute-done | bytes 196640 | tf_op jit(solution)/shard_map/ppermute | solution.py:407
  9.1 0.1 add_convert_fusion
  9.2 15.7 %all_to_all.5 = bf16[32,24,128]{2,1,0:T(8,128)(2,1)S(1)} all-to-all(bf16[32,24,128]{2,1,0:T(8,128)(2,1)S(1)} %bitcast.9), channel_id=1, replica_groups={{0,1,2,3,6,7,4,5,12,13,14,15,10,11,8,9,16,17,18,19,22,23,20,21,28,29,30..., dimensions={0} | all-to-all | bytes 393216 | tf_op jit(solution)/shard_map/all_to_all | solution.py:409
  24.9 1.1 %shard_map.65 = f32[768,12]{1,0:T(8,128)} custom-call(bf16[16,48,128]{2,1,0:T(8,128)(2,1)S(1)} %bitcast.7), custom_call_target="tpu_custom_call" | custom-call | tf_op jit(solution)/shard_map/pallas_call | solution.py:337
Async XLA Ops:
  7.6 1.6 %collective-permute-start = (bf16[16,48,128]{2,1,0:T(8,128)(2,1)S(1)}, bf16[16,48,128]{2,1,0:T(8,128)(2,1)S(1)}, u32[]{:S(2)}, u32[]{:S(2)}) collective-permute-start(bf16[16,48,128]{2,1,0:T(8,128)(2,1)S(1)} %get-tuple-element.8), channel_id=1, source_target_pairs={{0,1},{1,0},{2,3},{3,2},{4,5},{5,4},{6,7},{7,6},{8,9},{9,8},{10,11... | collective-permute-start | bytes 589832 | tf_op jit(solution)/shard_map/ppermute | solution.py:407
